TPU v7x, 512 devices: a whole 4x4x16 slice. The times are simulated.
512 devices in a mesh: dp: 16 (over x, y), cent: 32 (over z, core).
Axes of the slice: x: 4, y: 4, z: 16, core: 2. Of those that a mesh axis runs over, the one named last changes fastest.
Arguments:
- embeddings: bfloat16 [32768, 768], P(('dp', 'cent')), may hold values from -60 to 60, as said below
- candidates: int32 [32768, 32], P('dp'), may hold values from 0 to 255, all different within a row
- centroids: bfloat16 [32768, 768], P('cent'), may hold values from -5 to 7, as said below
Outputs:
- new_centroids: float32 [32768, 768], P('cent', 'dp')
Inputs may be any that keep to these rules, and one draw needn't show every extreme that they name: Real-valued embeddings. Real-valued centroids. `candidates`: each row lists 32 different blocks; every block is listed by some row.
All inputs are finite; a program needn't handle non-finite values.
Results may differ from a plain program's by a relative error of at most 0.0003.
Values may be sent and summed in bfloat16 or wider, within the bound.
A program may use at most 64 MiB of HBM per device.

v0:
```python
import math

import jax
import jax.numpy as jnp
from jax import lax
from jax.sharding import PartitionSpec as P

D = 768
BLOCK = 128


masked_value = -1e30


def on_device(embeddings, candidates, centroids):
    gathered = lax.all_gather(embeddings, "cent", axis=0, tiled=True)
    row_total_count = gathered.shape[0]
    local_rows = centroids.shape[0]
    block_count = local_rows // BLOCK
    score_scale = 1.0 / math.sqrt(D)
    owned_blocks = lax.axis_index("cent") * block_count + jnp.arange(block_count, dtype=jnp.int32)
    has_block = jnp.any(candidates[:, :, None] == owned_blocks[None, None, :], axis=1)
    products = lax.dot_general(
        gathered, centroids, (((1,), (1,)), ((), ())), preferred_element_type=jnp.float32
    )
    cent_f32 = centroids.astype(jnp.float32)
    half_sq = 0.5 * jnp.sum(cent_f32 * cent_f32, axis=1)
    logits = ((products - half_sq[None, :]) * score_scale).reshape(
        row_total_count, block_count, BLOCK
    )
    logits = jnp.where(has_block[:, :, None], logits, masked_value)
    local_max = jnp.max(logits, axis=(1, 2))
    row_max = lax.pmax(local_max, "cent")
    exponent = jnp.where(has_block[:, :, None], jnp.exp(logits - row_max[:, None, None]), 0.0)
    row_total = lax.psum(jnp.sum(exponent, axis=(1, 2)), "cent")
    weights = (exponent / row_total[:, None, None]).reshape(row_total_count, local_rows)
    total_mass = lax.psum(jnp.sum(weights, axis=0), "dp")
    weights_bf = weights.astype(jnp.bfloat16)
    sums = lax.dot_general(
        weights_bf, gathered, (((0,), (0,)), ((), ())), preferred_element_type=jnp.float32
    )
    partial_sums = lax.psum_scatter(sums, "dp", scatter_dimension=1, tiled=True)
    col_width = partial_sums.shape[1]
    old_columns = lax.dynamic_slice_in_dim(cent_f32, lax.axis_index("dp") * col_width, col_width, 1)
    return (partial_sums + old_columns) / (total_mass[:, None] + 1.0)


def solution(mesh):
    placed = (P(("dp", "cent"), None), P("dp", None), P("cent", None))
    return jax.shard_map(
        on_device, mesh=mesh, in_specs=placed, out_specs=P("cent", "dp"), check_vma=False
    )
```

profile of v0, /device:TPU:6, one launch (start us, length us, event | category | flops | bytes accessed | tf_op | source)
XLA Modules:
  0.0 303.2 jit_solution(8104367815877615102)
XLA Ops:
  6.5 0.0 all-gather.2.cloned.1.call-start
  6.5 0.7 all-gather.2.cloned.1.call-update
  7.3 0.0 reduce-scatter.2.cloned.1.call-start
  7.3 1.7 copy.6
  9.0 1.3 compare_reduce_fusion
  10.3 0.4 multiply_reduce_fusion
  10.7 76.2 %all-gather.2.cloned.1.call-done = bf16[2048,768]{1,0:T(8,128)(2,1)} async-done(((bf16[64,768]{1,0:T(8,128)(2,1)}), bf16[2048,768]{1,0:T(8,128)(2,1)}) %all-gather.2.cloned.1.call-update) | async-done | bytes 3145744 | tf_op jit(solution)/shard_map/all_gather | solution.py:16
  86.9 9.2 %fusion = (f32[2048]{0:T(1024)S(1)}, f32[2048,1024]{0,1:T(8,128)}) fusion(f32[1024]{0:T(1024)S(1)} %broadcast_multiply_fusion, pred[2048,8]{0,1:T(8,128)(4,1)S(1)} %compare_reduce_fusion, bf16[2048,768]{1,0:T(8,128)(2,1)} %all-gather.2.cloned.1.call-done, bf16[1024,768]{1,0:T(8,128)(2,1)} %param.5), kind=kOutput, calls=%fused_computation.2 | convolution fusion | flops 3229612032 | bytes 13135872 | tf_op jit(solution)/shard_map/dot_general | solution.py:23
  96.1 49.3 %pmax.7 = f32[2048]{0:T(1024)S(1)} all-reduce(f32[2048]{0:T(1024)S(1)} %get-tuple-element.7), channel_id=1, replica_groups=mesh['dp'=16,'cent'=32] {'cent'}, use_global_device_ids=true, to_apply=%region_3.4 | all-reduce | flops 2048 | bytes 16384 | tf_op jit(solution)/shard_map/pmax | solution.py:33
  145.4 4.9 %fusion.2 = f32[2048]{0:T(1024)S(1)} fusion(f32[2048,1024]{0,1:T(8,128)} %get-tuple-element.8, f32[2048]{0:T(1024)S(1)} %pmax.7, f32[1024]{0:T(1024)S(1)} %broadcast_multiply_fusion, pred[2048,8]{0,1:T(8,128)(4,1)S(1)} %compare_reduce_fusion), kind=kLoop, calls=%fused_computation.4 | loop fusion | flops 12580864 | bytes 8425472 | tf_op jit(solution)/shard_map/reduce_sum | solution.py:35
  150.3 46.8 %psum.14 = f32[2048]{0:T(1024)S(1)} all-reduce(f32[2048]{0:T(1024)S(1)} %fusion.2), channel_id=1, replica_groups=mesh['dp'=16,'cent'=32] {'cent'}, use_global_device_ids=true, to_apply=%region_5.6 | all-reduce | flops 2048 | bytes 16384 | tf_op jit(solution)/shard_map/psum | solution.py:35
  197.1 0.0 copy-start
  197.1 5.8 %fusion.5 = (f32[1024]{0:T(1024)S(1)}, bf16[2048,1024]{0,1:T(8,128)(2,1)S(1)}) fusion(f32[2048]{0:T(1024)S(1)} %psum.14, f32[2048]{0:T(1024)S(1)} %pmax.7, f32[2048,1024]{0,1:T(8,128)} %get-tuple-element.8, f32[1024]{0:T(1024)S(1)} %broadcast_multiply_fusion, pred[2048,8]{0,1:T(8,128)(4,1)S(1)} %compare_reduce_fusion), kind=kLoop, calls=%fused_computation.13 | loop fusion | flops 16776192 | bytes 12623872 | tf_op jit(solution)/shard_map/reduce_sum | solution.py:37
  202.9 0.0 copy-done
  202.9 5.3 %fusion.3 = f32[1024,768]{0,1:T(8,128)} fusion(bf16[2048,768]{1,0:T(8,128)(2,1)S(1)} %copy-done, bf16[2048,1024]{0,1:T(8,128)(2,1)S(1)} %get-tuple-element.6), kind=kOutput, calls=%fused_computation.5 | convolution fusion | flops 3221225472 | bytes 10485760 | tf_op jit(solution)/shard_map/dot_general | solution.py:39
  208.2 0.0 reduce-scatter.2.cloned.1.call-update
  208.2 2.1 convert_element_type.6
  210.3 33.7 %psum.15 = f32[1024]{0:T(1024)S(1)} all-reduce(f32[1024]{0:T(1024)S(1)} %get-tuple-element.5), channel_id=1, replica_groups=mesh['dp'=16,'cent'=32] {'dp'}, use_global_device_ids=true, to_apply=%region_8.9 | all-reduce | flops 1024 | bytes 8192 | tf_op jit(solution)/shard_map/psum | solution.py:37
  244.0 50.7 %reduce-scatter.2.cloned.1.call-done = f32[1024,48]{0,1:T(8,128)} async-done(((f32[1024,768]{0,1:T(8,128)}), f32[1024,48]{0,1:T(8,128)}) %reduce-scatter.2.cloned.1.call-update) | async-done | bytes 196624 | tf_op jit(solution)/shard_map/reduce_scatter | solution.py:42
  294.7 1.7 add_divide_fusion
  (3 shorter events, 0.0 us)
Async XLA Ops:
  6.5 80.4 %all-gather.2.cloned.1.call-start = ((), (), s32[]{:S(2)}) async-start(), calls=%async_computation.1 | async-start | bytes 3244032 | tf_op jit(solution)/shard_map/all_gather | solution.py:16
  7.3 287.4 %reduce-scatter.2.cloned.1.call-start = ((), (), s32[]{:S(2)}) async-start(), calls=%async_computation.2 | async-start | bytes 3342336 | tf_op jit(solution)/shard_map/reduce_scatter | solution.py:42
  197.1 5.8 %copy-start = (bf16[2048,768]{1,0:T(8,128)(2,1)S(1)}, bf16[2048,768]{1,0:T(8,128)(2,1)}, u32[]{:S(2)}) copy-start(bf16[2048,768]{1,0:T(8,128)(2,1)} %all-gather.2.cloned.1.call-done) | copy-start | bytes 9437188
Sparse Core Ops, SparseCore 0:
  9.5 77.4 all-gather.1
  208.3 86.2 reduce-scatter.1
where the time goes:
time: 304 us; the launch traced here: 303 us
  blocking collectives  130 us (43%)
  waiting for transfers between devices  128 us (42%)
  other arithmetic  16.2 us (5%)
  matrix products  14.4 us (5%)
  between operations  13.5 us (4%)
    all_gather x1, waiting for transfers between devices, on_device(): gathered = lax.all_gather(embeddings, 'cent', axis=0, tiled=True)  76.2 us
    reduce_scatter x1, waiting for transfers between devices, on_device(): partial_sums = lax.psum_scatter(sums, 'dp', scatter_dimension=1, tiled=True)  50.7 us
    pmax x1, blocking collectives, on_device(): row_max = lax.pmax(local_max, 'cent')  49.3 us
    psum x1, blocking collectives, on_device(): row_total = lax.psum(jnp.sum(exponent, axis=(1, 2)), 'cent')  46.8 us
    psum x1, blocking collectives, on_device(): total_mass = lax.psum(jnp.sum(weights, axis=0), 'dp')  33.7 us
    dot_general x1, matrix products, on_device(): lax.dot_general(gathered, centroids, (((1,), (1,)), ((), ())), preferred_...  9.15 us
  transfers between devices with their start and end apart: 2, of which 2 were waited for; matrix products, arithmetic and copies ran while one was open for 2% of the time, Pallas kernels for 0%

commit v1 on v0

v1 whole, which is shorter than its diff:
```python
import math

import jax
import jax.numpy as jnp
from jax import lax
from jax.experimental import pallas as pl
from jax.experimental.pallas import tpu as pltpu
from jax.sharding import PartitionSpec as P

D = 768
BLOCK = 128
Z = 16
SIDE = 4
SHARD = 64
CHUNK = 128
ROWS = Z * CHUNK
OWN = 1024
NBLK = OWN // BLOCK
COLS = 48
QN = 4
QW = OWN // QN
NCAND = 32
LOW = -1e30
FLOOR = -1e29
MESH = pl.DeviceIdType.MESH
NT = (((1,), (1,)), ((), ()))


def rem(a, b):
    return lax.rem(a, b)


def kernel(emb_hbm, cand_hbm, cent_hbm, out_ref,
           e_all, et, cent, cand, candt, hs, x_buf, w_buf, st, sb, fr, fac,
           mp, mass, mx, my, s_buf, rel1, dir1, rrl1, tmp1, r1, rel2, dir2, rrl2, tmp2, res,
           in_sem, ag_send, ag_recv, sib_send, sib_recv, st_send, st_recv, fr_send, fr_recv,
           m_send, m_recv, rs_send, rs_recv):
    dp = lax.axis_index("dp")
    ce = lax.axis_index("cent")
    z = ce // 2
    core = rem(ce, 2)
    px = dp // SIDE
    py = rem(dp, SIDE)
    right = rem(z + 1, Z)
    left = rem(z + Z - 1, Z)
    own = pl.ds(pl.multiple_of(core * SHARD, SHARD), SHARD)

    def dev(d, c):
        return (d, c)

    load_e = pltpu.make_async_copy(emb_hbm, e_all.at[0, own], in_sem.at[0])
    load_c = pltpu.make_async_copy(cent_hbm, cent, in_sem.at[1])
    load_k = pltpu.make_async_copy(cand_hbm, cand, in_sem.at[2])
    load_e.start()
    load_c.start()
    load_k.start()

    barrier = pltpu.get_barrier_semaphore()

    def greet_z(i, carry):
        pl.semaphore_signal(barrier, inc=1, device_id=dev(dp, rem(ce + i, 2 * Z)), device_id_type=MESH)
        return carry

    def greet_xy(k, carry):
        pl.semaphore_signal(barrier, inc=1, device_id=dev(rem(px + k, SIDE) * SIDE + py, ce), device_id_type=MESH)
        pl.semaphore_signal(barrier, inc=1, device_id=dev(px * SIDE + rem(py + k, SIDE), ce), device_id_type=MESH)
        return carry

    lax.fori_loop(1, 2 * Z, greet_z, 0)
    lax.fori_loop(1, SIDE, greet_xy, 0)
    pl.semaphore_wait(barrier, 2 * Z - 1 + 2 * (SIDE - 1))

    def hop(src, dst, rows, to_z):
        return pltpu.make_async_remote_copy(
            src_ref=e_all.at[src, rows], dst_ref=e_all.at[dst, rows],
            send_sem=ag_send.at[dst], recv_sem=ag_recv.at[dst],
            device_id=dev(dp, to_z * 2 + core), device_id_type=MESH)

    half_a = pl.ds(pl.multiple_of(core * SHARD, SHARD // 2), SHARD // 2)
    half_b = pl.ds(pl.multiple_of(core * SHARD + SHARD // 2, SHARD // 2), SHARD // 2)

    def hop_half(src, rows, sem, to_z):
        return pltpu.make_async_remote_copy(
            src_ref=e_all.at[src, rows], dst_ref=e_all.at[Z - 1, rows],
            send_sem=ag_send.at[sem], recv_sem=ag_recv.at[sem],
            device_id=dev(dp, to_z * 2 + core), device_id_type=MESH)

    def to_sibling(slot, rows):
        return pltpu.make_async_remote_copy(
            src_ref=e_all.at[slot, rows], dst_ref=e_all.at[slot, rows],
            send_sem=sib_send.at[slot], recv_sem=sib_recv.at[slot],
            device_id=dev(dp, z * 2 + 1 - core), device_id_type=MESH)

    other = pl.ds(pl.multiple_of((1 - core) * SHARD, SHARD), SHARD)

    load_e.wait()
    hop(0, 1, own, right).start()
    hop(0, 2, own, left).start()
    to_sibling(0, own).start()

    load_k.wait()
    for k in range(Z):
        part = cand[k * CHUNK:(k + 1) * CHUNK, :]
        wide = jnp.concatenate([part, jnp.zeros((CHUNK, BLOCK - NCAND), jnp.int32)], axis=1)
        candt[:, k * CHUNK:(k + 1) * CHUNK] = jnp.transpose(wide)[0:NCAND, :]
    load_c.wait()

    def square(b, carry):
        at = pl.ds(pl.multiple_of(b * BLOCK, BLOCK), BLOCK)
        c32 = cent[at, :].astype(jnp.float32)
        half = 0.5 * jnp.sum(c32 * c32, axis=1, keepdims=True)
        hs[at, :] = jnp.broadcast_to(half, (BLOCK, CHUNK))
        return carry

    lax.fori_loop(0, NBLK, square, 0)

    def source(i):
        odd = rem(i, 2)
        return rem(z + (1 - 2 * odd) * ((i + 1) // 2) + Z, Z)

    def holder(i):
        odd = rem(i, 2)
        return rem(z - (1 - 2 * odd) * ((i + 1) // 2) + Z, Z)

    def give_stats(i, c):
        return pltpu.make_async_remote_copy(
            src_ref=st.at[i], dst_ref=sb.at[2 * i + core],
            send_sem=st_send.at[2 * i + c], recv_sem=st_recv.at[2 * i + core],
            device_id=dev(dp, source(i) * 2 + c), device_id_type=MESH)

    scale = 1.0 / math.sqrt(D)

    def chunk(i, carry):
        to_sibling(i, other).wait_recv()
        lanes = pl.ds(pl.multiple_of(i * CHUNK, CHUNK), CHUNK)
        e = e_all[i]
        et[:, lanes] = jnp.transpose(e)
        listed = candt[:, pl.ds(pl.multiple_of(source(i) * CHUNK, CHUNK), CHUNK)]
        top = jnp.full((8, CHUNK), FLOOR, jnp.float32)
        for b in range(NBLK):
            dots = lax.dot_general(cent[b * BLOCK:(b + 1) * BLOCK, :], e, NT, preferred_element_type=jnp.float32)
            hit = jnp.max(jnp.where(listed == ce * NBLK + b, 1.0, 0.0), axis=0, keepdims=True)
            l = (dots - hs[b * BLOCK:(b + 1) * BLOCK, :]) * scale
            l = jnp.where(hit > 0.5, l, LOW)
            x_buf[b * BLOCK:(b + 1) * BLOCK, lanes] = l
            top = jnp.maximum(top, jnp.max(l.reshape(BLOCK // 8, 8, CHUNK), axis=0))
        m = jnp.max(top, axis=0, keepdims=True)
        total = jnp.zeros((8, CHUNK), jnp.float32)
        for b in range(NBLK):
            ex = jnp.exp(x_buf[b * BLOCK:(b + 1) * BLOCK, lanes] - m)
            x_buf[b * BLOCK:(b + 1) * BLOCK, lanes] = ex
            total = total + jnp.sum(ex.reshape(BLOCK // 8, 8, CHUNK), axis=0)
        st[i, 0:1] = m
        st[i, 1:2] = jnp.sum(total, axis=0, keepdims=True)

        @pl.when(i == 0)
        def _():
            sb[core] = st[0]
            give_stats(i, 1 - core).start()

        @pl.when(i > 0)
        def _():
            give_stats(i, 0).start()
            give_stats(i, 1).start()

        return carry

    def step(s, carry):
        @pl.when(s <= 7)
        def _():
            hop(2 * s - 1, 2 * s - 1, own, right).wait_recv()

            @pl.when(s <= 6)
            def _():
                hop(2 * s - 1, 2 * s + 1, own, right).start()

            @pl.when(s == 7)
            def _():
                hop_half(13, half_a, 15, right).start()

            to_sibling(2 * s - 1, own).start()
            hop(2 * s, 2 * s, own, left).wait_recv()

            @pl.when(s <= 6)
            def _():
                hop(2 * s, 2 * s + 2, own, left).start()

            @pl.when(s == 7)
            def _():
                hop_half(14, half_b, 16, left).start()

            to_sibling(2 * s, own).start()

        @pl.when(s == 8)
        def _():
            hop_half(15, half_a, 15, right).wait_recv()
            hop_half(15, half_b, 16, left).wait_recv()
            to_sibling(15, own).start()

        lax.fori_loop(jnp.maximum(2 * s - 3, 0), jnp.minimum(2 * s - 1, Z), chunk, 0)
        return carry

    lax.fori_loop(1, 10, step, 0)

    def take_stats(k, carry):
        @pl.when(k != core)
        def _():
            pltpu.make_async_remote_copy(
                src_ref=st.at[0], dst_ref=sb.at[k], send_sem=st_send.at[k], recv_sem=st_recv.at[k],
                device_id=dev(dp, z * 2 + 1 - core), device_id_type=MESH).wait_recv()
        return carry

    lax.fori_loop(0, 2 * Z, take_stats, 0)
    big = jnp.full((1, CHUNK), FLOOR, jnp.float32)
    for k in range(2 * Z):
        big = jnp.maximum(big, sb[k, 0:1])
    tot = jnp.zeros((1, CHUNK), jnp.float32)
    for k in range(2 * Z):
        tot = tot + sb[k, 1:2] * jnp.exp(sb[k, 0:1] - big)
    fr[0, 0:1] = big
    fr[0, 1:2] = 1.0 / tot

    def hand_out(i):
        return pltpu.make_async_remote_copy(
            src_ref=fr.at[0], dst_ref=fr.at[i], send_sem=fr_send.at[i], recv_sem=fr_recv.at[i],
            device_id=dev(dp, holder(i) * 2 + core), device_id_type=MESH)

    def send_out(k, carry):
        hand_out(Z - k).start()
        return carry

    lax.fori_loop(1, Z, send_out, 0)

    def factor(i, carry):
        @pl.when(i > 0)
        def _():
            hand_out(i).wait_recv()
        lanes = pl.ds(pl.multiple_of(i * CHUNK, CHUNK), CHUNK)
        fac[0:1, lanes] = jnp.exp(st[i, 0:1] - fr[i, 0:1]) * fr[i, 1:2]
        return carry

    lax.fori_loop(0, Z, factor, 0)

    def neighbour(q, stage, way):
        along_x = rem(q + stage + 1, 2)
        along_y = 1 - along_x
        nx = rem(px + way * along_x + SIDE, SIDE)
        ny = rem(py + way * along_y + SIDE, SIDE)
        return dev(nx * SIDE + ny, ce)

    def place(q, stage):
        along_x = rem(q + stage + 1, 2)
        return px * along_x + py * (1 - along_x)

    def rs(src, dst, q, stage, part, way):
        k = ((q * 2 + stage) * 3 + part) * 2 + way
        return pltpu.make_async_remote_copy(
            src_ref=src, dst_ref=dst, send_sem=rs_send.at[k], recv_sem=rs_recv.at[k],
            device_id=neighbour(q, stage, 1 - 2 * way), device_id_type=MESH)

    lo2, hi2 = pl.ds(0, 2), pl.ds(2, 2)
    loc, hic = pl.ds(0, COLS // 2), pl.ds(COLS // 2, COLS // 2)

    def shift(a, k):
        return rem(a + k, SIDE)

    def first(q):
        a = place(q, 0)
        return [
            rs(s_buf.at[q, shift(a, 2), lo2], rel1.at[q, 0], q, 0, 0, 0),
            rs(s_buf.at[q, shift(a, 2), hi2], rel1.at[q, 1], q, 0, 0, 1),
            rs(s_buf.at[q, shift(a, 1), hi2], dir1.at[q, 0], q, 0, 1, 0),
            rs(s_buf.at[q, shift(a, 3), lo2], dir1.at[q, 1], q, 0, 1, 1),
        ]

    def second(q):
        return [
            rs(tmp1.at[q, 0], rrl1.at[q, 0], q, 0, 2, 0),
            rs(tmp1.at[q, 1], rrl1.at[q, 1], q, 0, 2, 1),
        ]

    def third(q):
        b = place(q, 1)
        return [
            rs(r1.at[q, shift(b, 2), loc], rel2.at[q, 0], q, 1, 0, 0),
            rs(r1.at[q, shift(b, 2), hic], rel2.at[q, 1], q, 1, 0, 1),
            rs(r1.at[q, shift(b, 1), hic], dir2.at[q, 0], q, 1, 1, 0),
            rs(r1.at[q, shift(b, 3), loc], dir2.at[q, 1], q, 1, 1, 1),
        ]

    def fourth(q):
        return [
            rs(tmp2.at[q, 0], rrl2.at[q, 0], q, 1, 2, 0),
            rs(tmp2.at[q, 1], rrl2.at[q, 1], q, 1, 2, 1),
        ]

    SUB = 32

    def add_up(q, carry):
        def weigh(r, c):
            at = pl.ds(pl.multiple_of(q * QW + r * SUB, SUB), SUB)
            w = x_buf[at, :] * fac[0:1, :]
            w_buf[pl.ds(pl.multiple_of(r * SUB, SUB), SUB), :] = w.astype(jnp.bfloat16)
            part = w[:, 0:128]
            for k in range(1, ROWS // 128):
                part = part + w[:, k * 128:(k + 1) * 128]
            mp[at, :] = part
            return c

        lax.fori_loop(0, QW // SUB, weigh, 0)
        swap = rem(q, 2)

        def tall(g, c):
            rows = pl.ds(pl.multiple_of(g * 384, 128), 384)
            y = lax.dot_general(et[rows, :], w_buf[...], NT, preferred_element_type=jnp.float32)
            for j in range(8):
                jx = g * 2 + j // 4
                jy = j % 4
                i0 = jx + swap * (jy - jx)
                i1 = jy + swap * (jx - jy)
                s_buf[q, i0, i1] = y[j * COLS:(j + 1) * COLS, :]
            return c

        lax.fori_loop(0, 2, tall, 0)
        for copy in first(q):
            copy.start()
        return carry

    lax.fori_loop(0, QN, add_up, 0)

    def mass_copy(src, dst, stage, k):
        along_x = 1 - stage
        nx = rem(px + k * along_x, SIDE)
        ny = rem(py + k * stage, SIDE)
        return pltpu.make_async_remote_copy(
            src_ref=src, dst_ref=dst.at[k], send_sem=m_send.at[stage * SIDE + k], recv_sem=m_recv.at[stage * SIDE + k],
            device_id=dev(nx * SIDE + ny, ce), device_id_type=MESH)

    for k in range(NBLK):
        turned = jnp.transpose(mp[k * 128:(k + 1) * 128, :])
        mx[0, 0:1, k * 128:(k + 1) * 128] = jnp.sum(turned, axis=0, keepdims=True)
    for k in range(1, SIDE):
        mass_copy(mx.at[0], mx, 0, k).start()

    def relay1(q, carry):
        a = place(q, 0)
        for copy in first(q)[0:2]:
            copy.wait_recv()
        tmp1[q, 0] = rel1[q, 0] + s_buf[q, shift(a, 1), lo2]
        tmp1[q, 1] = rel1[q, 1] + s_buf[q, shift(a, 3), hi2]
        for copy in second(q):
            copy.start()
        return carry

    lax.fori_loop(0, QN, relay1, 0)

    pick_r = lax.broadcasted_iota(jnp.int32, (COLS, D), 0)
    pick_c = lax.broadcasted_iota(jnp.int32, (COLS, D), 1)
    pick = jnp.where(pick_c == pick_r + dp * COLS, 1.0, 0.0).astype(jnp.bfloat16)
    for b in range(NBLK // 2):
        at = slice(b * QW, (b + 1) * QW)
        res[b] = lax.dot_general(pick, cent[at, :], NT, preferred_element_type=jnp.float32)

    for k in range(1, SIDE):
        mass_copy(mx.at[0], mx, 0, k).wait_recv()
    my[0] = (mx[0] + mx[1]) + (mx[2] + mx[3])
    for k in range(1, SIDE):
        mass_copy(my.at[0], my, 1, k).start()

    def close1(q, carry):
        a = place(q, 0)
        for copy in first(q)[2:4] + second(q):
            copy.wait_recv()
        r1[q, 0:2] = s_buf[q, a, lo2] + dir1[q, 1] + rrl1[q, 0]
        r1[q, 2:4] = s_buf[q, a, hi2] + dir1[q, 0] + rrl1[q, 1]
        for copy in third(q):
            copy.start()
        return carry

    lax.fori_loop(0, QN, close1, 0)

    def relay2(q, carry):
        b = place(q, 1)
        for copy in third(q)[0:2]:
            copy.wait_recv()
        tmp2[q, 0] = rel2[q, 0] + r1[q, shift(b, 1), loc]
        tmp2[q, 1] = rel2[q, 1] + r1[q, shift(b, 3), hic]
        for copy in fourth(q):
            copy.start()
        return carry

    lax.fori_loop(0, QN, relay2, 0)

    for k in range(1, SIDE):
        mass_copy(my.at[0], my, 1, k).wait_recv()
    mass[...] = 1.0 / ((my[0] + my[1]) + (my[2] + my[3]) + 1.0)

    def close2(q, carry):
        b = place(q, 1)
        for copy in third(q)[2:4] + fourth(q):
            copy.wait_recv()
        lanes = pl.ds(pl.multiple_of(q * QW, QW), QW)
        inv = mass[0:1, lanes]
        out_ref[0:24, lanes] = (r1[q, b, loc] + dir2[q, 1] + rrl2[q, 0] + res[q, 0:24]) * inv
        out_ref[24:48, lanes] = (r1[q, b, hic] + dir2[q, 0] + rrl2[q, 1] + res[q, 24:48]) * inv
        return carry

    lax.fori_loop(0, QN, close2, 0)

    def sent_q(q, carry):
        for copy in first(q) + second(q) + third(q) + fourth(q):
            copy.wait_send()
        return carry

    lax.fori_loop(0, QN, sent_q, 0)
    for k in range(1, SIDE):
        mass_copy(mx.at[0], mx, 0, k).wait_send()
        mass_copy(my.at[0], my, 1, k).wait_send()

    def sent_z(i, carry):
        to_sibling(i, own).wait_send()

        @pl.when(i > 0)
        def _():
            give_stats(i, 0).wait_send()
            give_stats(i, 1).wait_send()
            hand_out(i).wait_send()

            @pl.when(i < Z - 1)
            def _():
                hop(i, i, own, right).wait_send()
        return carry

    lax.fori_loop(0, Z, sent_z, 0)
    give_stats(0, 1 - core).wait_send()
    hop_half(13, half_a, 15, right).wait_send()
    hop_half(14, half_b, 16, left).wait_send()


def on_device(embeddings, candidates, centroids):
    f32, bf16 = jnp.float32, jnp.bfloat16
    dma = pltpu.SemaphoreType.DMA
    turned = pl.pallas_call(
        kernel,
        out_shape=jax.ShapeDtypeStruct((COLS, OWN), f32),
        in_specs=[pl.BlockSpec(memory_space=pl.ANY)] * 3,
        out_specs=pl.BlockSpec(memory_space=pltpu.VMEM),
        scratch_shapes=[
            pltpu.VMEM((Z, CHUNK, D), bf16),
            pltpu.VMEM((D, ROWS), bf16),
            pltpu.VMEM((OWN, D), bf16),
            pltpu.VMEM((ROWS, NCAND), jnp.int32),
            pltpu.VMEM((NCAND, ROWS), jnp.int32),
            pltpu.VMEM((OWN, CHUNK), f32),
            pltpu.VMEM((OWN, ROWS), f32),
            pltpu.VMEM((QW, ROWS), bf16),
            pltpu.VMEM((Z, 2, CHUNK), f32),
            pltpu.VMEM((2 * Z, 2, CHUNK), f32),
            pltpu.VMEM((Z, 2, CHUNK), f32),
            pltpu.VMEM((1, ROWS), f32),
            pltpu.VMEM((OWN, 128), f32),
            pltpu.VMEM((1, OWN), f32),
            pltpu.VMEM((SIDE, 1, OWN), f32),
            pltpu.VMEM((SIDE, 1, OWN), f32),
            pltpu.VMEM((QN, SIDE, SIDE, COLS, QW), f32),
            pltpu.VMEM((QN, 2, 2, COLS, QW), f32),
            pltpu.VMEM((QN, 2, 2, COLS, QW), f32),
            pltpu.VMEM((QN, 2, 2, COLS, QW), f32),
            pltpu.VMEM((QN, 2, 2, COLS, QW), f32),
            pltpu.VMEM((QN, SIDE, COLS, QW), f32),
            pltpu.VMEM((QN, 2, COLS // 2, QW), f32),
            pltpu.VMEM((QN, 2, COLS // 2, QW), f32),
            pltpu.VMEM((QN, 2, COLS // 2, QW), f32),
            pltpu.VMEM((QN, 2, COLS // 2, QW), f32),
            pltpu.VMEM((QN, COLS, QW), f32),
            dma((3,)),
            dma((Z + 1,)), dma((Z + 1,)),
            dma((Z,)), dma((Z,)),
            dma((2 * Z,)), dma((2 * Z,)),
            dma((Z,)), dma((Z,)),
            dma((2 * SIDE,)), dma((2 * SIDE,)),
            dma((QN * 12,)), dma((QN * 12,)),
        ],
        compiler_params=pltpu.CompilerParams(
            collective_id=0, has_side_effects=True, vmem_limit_bytes=56 * 1024 * 1024),
    )(embeddings, candidates, centroids)
    return jnp.transpose(turned)


def solution(mesh):
    placed = (P(("dp", "cent"), None), P("dp", None), P("cent", None))
    return jax.shard_map(
        on_device, mesh=mesh, in_specs=placed, out_specs=P("cent", "dp"), check_vma=False
    )
```

time: 304 us -> 97.2 us (0.32)
  blocking collectives: 130 us -> 0 us
  waiting for transfers between devices: 128 us -> 0 us
  Pallas kernels: 0 us -> 93.1 us
  other arithmetic: 16.2 us -> 0 us
  matrix products: 14.4 us -> 0 us
  between operations: 13.5 us -> 0.01 us
    pallas_call x0 -> x1, Pallas kernels: none -> 93.1 us  [on_device(): pl.pallas_call(kernel, out_shape=jax.ShapeDtypeStruct((COLS, OWN), f32),...]
    psum x2 -> x0, blocking collectives: 80.5 us -> none  [the longest x1 46.8 us: on_device(): row_total = lax.psum(jnp.sum(exponent, axis=(1, 2)), 'cent')]
    all_gather x1 -> x0, waiting for transfers between devices: 76.2 us -> none  [on_device(): gathered = lax.all_gather(embeddings, 'cent', axis=0, tiled=True)]
    reduce_scatter x1 -> x0, waiting for transfers between devices: 50.7 us -> none  [on_device(): partial_sums = lax.psum_scatter(sums, 'dp', scatter_dimension=1, tiled=True)]
    pmax x1 -> x0, blocking collectives: 49.3 us -> none  [on_device(): row_max = lax.pmax(local_max, 'cent')]
    dot_general x2 -> x0, matrix products: 14.4 us -> none  [the longest x1 9.15 us: on_device(): lax.dot_general(gathered, centroids, (((1,), (1,)), ((), ())), preferred_...]
    reduce_sum x3 -> x0, other arithmetic: 11 us -> none  [the longest x1 5.76 us: on_device(): total_mass = lax.psum(jnp.sum(weights, axis=0), 'dp')]
  transfers between devices with their start and end apart: 2 -> 0, of which waited for: 2 -> 0; matrix products, arithmetic and copies ran while one was open for 2% -> 0% of each run, Pallas kernels for 0% -> 0%
where the time goes in v1:
time: 97.2 us; the launch traced here: 97 us
  Pallas kernels  93.1 us (96%)
  local copies, waits for them, and re-layouts  3.9 us (4%)
    pallas_call x1, Pallas kernels, on_device(): pl.pallas_call(kernel, out_shape=jax.ShapeDtypeStruct((COLS, OWN), f32),...  93.1 us
    unnamed x2, local copies, waits for them, and re-layouts  3.9 us

profile of v1, /device:TPU:6, one launch (start us, length us, event | category | flops | bytes accessed | tf_op | source)
XLA Modules:
  0.0 97.0 jit_solution(8613939667670242994)
XLA Ops:
  0.0 2.3 %copy.4.cand_hbm = s32[2048,32]{1,0:T(8,128)} copy(s32[2048,32]{0,1:T(8,128)} %param.4) | data formatting | bytes 524288 | tf_op args[1]
  2.3 93.1 %shard_map.37 = f32[48,1024]{1,0:T(8,128)} custom-call(bf16[64,768]{1,0:T(8,128)(2,1)} %emb_hbm.1, s32[2048,32]{1,0:T(8,128)} %copy.4.cand_hbm, bf16[1024,768]{1,0:T(8,128)(2,1)} %cent_hbm.1), custom_call_target="tpu_custom_call" | custom-call | tf_op jit(solution)/shard_map/pallas_call | solution.py:443
  95.4 1.6 %copy.6 = f32[1024,48]{0,1:T(8,128)} copy(f32[1024,48]{0,1:T(8,128)} %bitcast.1) | data formatting | bytes 393216

commit v2 on v0

v2 whole, which is shorter than its diff:
```python
import math

import jax
import jax.numpy as jnp
from jax import lax
from jax.experimental import pallas as pl
from jax.experimental.pallas import tpu as pltpu
from jax.sharding import PartitionSpec as P

D = 768
BLOCK = 128
Z = 16
SIDE = 4
SHARD = 64
CHUNK = 128
ROWS = Z * CHUNK
OWN = 1024
NBLK = OWN // BLOCK
COLS = 48
QN = 4
QW = OWN // QN
NCAND = 32
LOW = -1e30
FLOOR = -1e29
MESH = pl.DeviceIdType.MESH
NT = (((1,), (1,)), ((), ()))
PIECE = 16
PIECES = SHARD // PIECE
NEAR = (1, -1, 2, -2)
STRIDE = (1, -1, 2, 0)
TOP = 32766.0
TINY = 1e-30


def rem(a, b):
    return lax.rem(a, b)


def kernel(emb_hbm, cand_hbm, cent_hbm, out_ref,
           e_all, et, cent, candt, hs, x_buf, w_buf, top_buf, tot_buf, st, sb, s2, s2r, fr, fac,
           mp, mass, mx, my, s_buf, s_q, rel1, dir1, rrl1, tmp1, sc1, sc1r, st1, st1r,
           r1, r_q, rel2, dir2, rrl2, tmp2, sc2, sc2r, st2, st2r, res,
           in_sem, ag_send, ag_recv, sib_send, sib_recv, st_send, st_recv, s2_send, s2_recv,
           m_send, m_recv, rs_send, rs_recv):
    f32 = jnp.float32
    dp = lax.axis_index("dp")
    ce = lax.axis_index("cent")
    z = ce // 2
    core = rem(ce, 2)
    px = dp // SIDE
    py = rem(dp, SIDE)
    right = rem(z + 1, Z)
    left = rem(z + Z - 1, Z)
    own = pl.ds(pl.multiple_of(core * SHARD, SHARD), SHARD)

    load_e = pltpu.make_async_copy(emb_hbm, e_all.at[0, own], in_sem.at[0])
    load_c = pltpu.make_async_copy(cent_hbm, cent, in_sem.at[1])
    load_k = pltpu.make_async_copy(cand_hbm, candt, in_sem.at[2])
    load_e.start()
    load_c.start()
    load_k.start()

    barrier = pltpu.get_barrier_semaphore()

    def greet(d, c):
        pl.semaphore_signal(barrier, inc=1, device_id=(d, c), device_id_type=MESH)

    for c in range(2):
        for away in NEAR:
            greet(dp, rem(z + away + Z, Z) * 2 + c)
    greet(dp, z * 2 + 1 - core)
    for k in range(1, SIDE):
        greet(rem(px + k, SIDE) * SIDE + py, ce)
        greet(px * SIDE + rem(py + k, SIDE), ce)
    pl.semaphore_wait(barrier, 2 * len(NEAR) + 1 + 2 * (SIDE - 1))

    def hop(src, dst, p, to_z):
        rows = pl.ds(pl.multiple_of(core * SHARD + p * PIECE, PIECE), PIECE)
        return pltpu.make_async_remote_copy(
            src_ref=e_all.at[src, rows], dst_ref=e_all.at[dst, rows],
            send_sem=ag_send.at[dst * PIECES + p], recv_sem=ag_recv.at[dst * PIECES + p],
            device_id=(dp, to_z * 2 + core), device_id_type=MESH)

    def to_sibling(slot, rows):
        return pltpu.make_async_remote_copy(
            src_ref=e_all.at[slot, rows], dst_ref=e_all.at[slot, rows],
            send_sem=sib_send.at[slot], recv_sem=sib_recv.at[slot],
            device_id=(dp, z * 2 + 1 - core), device_id_type=MESH)

    other = pl.ds(pl.multiple_of((1 - core) * SHARD, SHARD), SHARD)

    load_e.wait()
    for p in range(PIECES):
        hop(0, 1, p, right).start()
        hop(0, 2, p, left).start()
    to_sibling(0, own).start()

    load_k.wait()
    load_c.wait()

    def square(b, carry):
        at = pl.ds(pl.multiple_of(b * BLOCK, BLOCK), BLOCK)
        c32 = cent[at, :].astype(f32)
        half = 0.5 * jnp.sum(c32 * c32, axis=1, keepdims=True)
        hs[at, :] = jnp.broadcast_to(half, (BLOCK, CHUNK))
        return carry

    lax.fori_loop(0, NBLK, square, 0)

    def source(i):
        odd = rem(i, 2)
        return rem(z + (1 - 2 * odd) * ((i + 1) // 2) + Z, Z)

    def give_stats(i, j):
        zs = source(i)
        return pltpu.make_async_remote_copy(
            src_ref=st.at[zs], dst_ref=sb.at[j - 1, zs],
            send_sem=st_send.at[(j - 1) * Z + zs], recv_sem=st_recv.at[(j - 1) * Z + zs],
            device_id=(dp, rem(z + 4 * j, Z) * 2 + core), device_id_type=MESH)

    scale = 1.0 / math.sqrt(D)

    def listed(i):
        return candt[:, pl.ds(pl.multiple_of(source(i) * CHUNK, CHUNK), CHUNK)]

    def logits(b, e, blocks, lanes, top):
        width = e.shape[0]
        at = slice(b * BLOCK, (b + 1) * BLOCK)
        dots = lax.dot_general(cent[at, :], e, NT, preferred_element_type=f32)
        hit = jnp.max(jnp.where(blocks == ce * NBLK + b, 1.0, 0.0), axis=0, keepdims=True)
        h = hs[at, :]
        if width > CHUNK:
            h = jnp.concatenate([h, h], axis=1)
        l = jnp.where(hit > 0.5, (dots - h) * scale, LOW)
        x_buf[at, lanes] = l
        return jnp.maximum(top, jnp.max(l.reshape(BLOCK // 8, 8, width), axis=0))

    def powers(b, m, lanes, total):
        at = slice(b * BLOCK, (b + 1) * BLOCK)
        ex = jnp.exp(x_buf[at, lanes] - m)
        x_buf[at, lanes] = ex
        return total + jnp.sum(ex.reshape(BLOCK // 8, 8, m.shape[1]), axis=0)

    def single(i):
        to_sibling(i, other).wait_recv()
        lanes = pl.ds(pl.multiple_of(i * CHUNK, CHUNK), CHUNK)
        e = e_all[i]
        blocks = listed(i)
        top = jnp.full((8, CHUNK), FLOOR, f32)
        for b in range(NBLK):
            top = logits(b, e, blocks, lanes, top)
        m = jnp.max(top, axis=0, keepdims=True)
        total = jnp.zeros((8, CHUNK), f32)
        for b in range(NBLK):
            total = powers(b, m, lanes, total)
        zs = source(i)
        st[zs, 0:1] = m
        st[zs, 1:2] = jnp.sum(total, axis=0, keepdims=True)

    def pair(u, part):
        ia, ib = 2 * u - 1, 2 * u
        lanes = pl.ds(pl.multiple_of(ia * CHUNK, CHUNK), 2 * CHUNK)
        half = NBLK // 2
        if part == 0:
            to_sibling(ia, other).wait_recv()
            to_sibling(ib, other).wait_recv()
        if part < 2:
            e = e_all[pl.ds(ia, 2)].reshape(2 * CHUNK, D)
            blocks = jnp.concatenate([listed(ia), listed(ib)], axis=1)
            top = jnp.full((8, 2 * CHUNK), FLOOR, f32) if part == 0 else top_buf[...]
            for b in range(part * half, (part + 1) * half):
                top = logits(b, e, blocks, lanes, top)
            if part == 1:
                top = jnp.broadcast_to(jnp.max(top, axis=0, keepdims=True), top.shape)
            top_buf[...] = top
        else:
            m = top_buf[0:1, :]
            total = jnp.zeros((8, 2 * CHUNK), f32) if part == 2 else tot_buf[...]
            for b in range((part - 2) * half, (part - 1) * half):
                total = powers(b, m, lanes, total)
            i = ia if part == 2 else ib
            et[:, pl.ds(pl.multiple_of(i * CHUNK, CHUNK), CHUNK)] = jnp.transpose(e_all[i])
            if part == 2:
                tot_buf[...] = total
            else:
                t = jnp.sum(total, axis=0, keepdims=True)
                za, zb = source(ia), source(ib)
                st[za, 0:1] = m[:, :CHUNK]
                st[za, 1:2] = t[:, :CHUNK]
                st[zb, 0:1] = m[:, CHUNK:]
                st[zb, 1:2] = t[:, CHUNK:]

    HALF = PIECES // 2

    def step(s, carry):
        for p in range(PIECES):
            @pl.when(s <= 7)
            def _():
                hop(2 * s - 1, 2 * s - 1, p, right).wait_recv()

                @pl.when((s <= 6) | (p < HALF))
                def _():
                    hop(2 * s - 1, 2 * s + 1, p, right).start()

                hop(2 * s, 2 * s, p, left).wait_recv()

                @pl.when(s <= 6)
                def _():
                    hop(2 * s, 2 * s + 2, p, left).start()

                if p >= HALF:
                    @pl.when(s == 7)
                    def _():
                        hop(14, 15, p, left).start()

                if p == PIECES - 1:
                    to_sibling(2 * s - 1, own).start()
                    to_sibling(2 * s, own).start()

            if p == PIECES - 1:
                @pl.when(s == 8)
                def _():
                    for k in range(PIECES):
                        hop(15, 15, k, right).wait_recv()
                    to_sibling(15, own).start()

            @pl.when((s >= 2) & (s <= 8))
            def _():
                pair(s - 1, p)

        @pl.when((s == 1) | (s == 9))
        def _():
            i = jnp.where(s == 1, 0, Z - 1)
            single(i)
            et[:, pl.ds(pl.multiple_of(i * CHUNK, CHUNK), CHUNK)] = jnp.transpose(e_all[i])

        def tell(i, c):
            give_stats(i, 1).start()
            give_stats(i, 3).start()
            return c

        def tell_far(i, c):
            give_stats(i, 2).start()
            return c

        @pl.when(s >= 4)
        def _():
            lax.fori_loop(jnp.where(s == 4, 0, 2 * s - 3), jnp.minimum(2 * s - 1, Z), tell, 0)

        @pl.when(s >= 8)
        def _():
            lax.fori_loop(jnp.where(s == 8, 0, 15), jnp.minimum(2 * s - 1, Z), tell_far, 0)

        return carry

    lax.fori_loop(1, 10, step, 0)

    def take_stats(k, carry):
        for j in range(1, SIDE):
            give_stats(k, j).wait_recv()
        return carry

    lax.fori_loop(0, Z, take_stats, 0)

    def merge(parts):
        big = parts[0][0]
        for m, _ in parts[1:]:
            big = jnp.maximum(big, m)
        tot = None
        for m, t in parts:
            term = t * jnp.exp(m - big)
            tot = term if tot is None else tot + term
        return big, tot

    big, tot = merge([(st[:, 0, :], st[:, 1, :])] + [(sb[j, :, 0, :], sb[j, :, 1, :]) for j in range(SIDE - 1)])
    s2[:, 0, :] = big
    s2[:, 1, :] = tot

    def share(k, c):
        return pltpu.make_async_remote_copy(
            src_ref=s2, dst_ref=s2r.at[2 * k + core],
            send_sem=s2_send.at[2 * k + c], recv_sem=s2_recv.at[2 * k + core],
            device_id=(dp, rem(z + STRIDE[k] + Z, Z) * 2 + c), device_id_type=MESH)

    def take_share(k, c):
        return pltpu.make_async_remote_copy(
            src_ref=s2, dst_ref=s2r.at[2 * k + c],
            send_sem=s2_send.at[2 * k + c], recv_sem=s2_recv.at[2 * k + c],
            device_id=(dp, z * 2 + 1 - core), device_id_type=MESH)

    for k in range(3):
        share(k, 0).start()
        share(k, 1).start()
    share(3, 1 - core).start()
    for k in range(3):
        take_share(k, 0).wait_recv()
        take_share(k, 1).wait_recv()
    take_share(3, 1 - core).wait_recv()
    big, tot = merge(
        [(s2[:, 0, :], s2[:, 1, :]), (s2r[6 + 1 - core, :, 0, :], s2r[6 + 1 - core, :, 1, :])]
        + [(s2r[k, :, 0, :], s2r[k, :, 1, :]) for k in range(6)])
    fr[:, 0, :] = jnp.exp(st[:, 0, :] - big) / tot

    def factor(i, carry):
        fac[0:1, pl.ds(pl.multiple_of(i * CHUNK, CHUNK), CHUNK)] = fr[source(i)]
        return carry

    lax.fori_loop(0, Z, factor, 0)

    def neighbour(q, stage, way):
        along_x = rem(q + stage + 1, 2)
        along_y = 1 - along_x
        nx = rem(px + way * along_x + SIDE, SIDE)
        ny = rem(py + way * along_y + SIDE, SIDE)
        return (nx * SIDE + ny, ce)

    def place(q, stage):
        along_x = rem(q + stage + 1, 2)
        return px * along_x + py * (1 - along_x)

    def rs(src, dst, q, stage, part, way):
        k = ((q * 2 + stage) * 5 + part) * 2 + way
        return pltpu.make_async_remote_copy(
            src_ref=src, dst_ref=dst, send_sem=rs_send.at[k], recv_sem=rs_recv.at[k],
            device_id=neighbour(q, stage, 1 - 2 * way), device_id_type=MESH)

    la, lb = slice(0, 128), slice(128, 256)
    da, db = pl.ds(0, 128), pl.ds(128, 128)

    def shift(a, k):
        return rem(a + k, SIDE)

    def opening(q, stage):
        a = place(q, stage)
        x, rel, dr, sc, scr = (s_q, rel1, dir1, sc1, sc1r) if stage == 0 else (r_q, rel2, dir2, sc2, sc2r)
        mid = (slice(None), slice(None)) if stage == 0 else (slice(None),)

        def piece(k, lanes):
            return x.at[(q, shift(a, k)) + mid + (lanes,)]
        return [
            rs(sc.at[q], scr.at[q, 0], q, stage, 3, 0),
            rs(sc.at[q], scr.at[q, 1], q, stage, 3, 1),
            rs(piece(2, da), rel.at[q, 0], q, stage, 0, 0),
            rs(piece(2, db), rel.at[q, 1], q, stage, 0, 1),
            rs(piece(1, db), dr.at[q, 0], q, stage, 1, 0),
            rs(piece(3, da), dr.at[q, 1], q, stage, 1, 1),
        ]

    def closing(q, stage):
        tmp, rrl, sc, scr = (tmp1, rrl1, st1, st1r) if stage == 0 else (tmp2, rrl2, st2, st2r)
        return [
            rs(sc.at[q, 0], scr.at[q, 0], q, stage, 4, 0),
            rs(sc.at[q, 1], scr.at[q, 1], q, stage, 4, 1),
            rs(tmp.at[q, 0], rrl.at[q, 0], q, stage, 2, 0),
            rs(tmp.at[q, 1], rrl.at[q, 1], q, stage, 2, 1),
        ]

    def peak(v, high):
        return jnp.maximum(high, jnp.max(jnp.abs(v).reshape(COLS // 8, 8, v.shape[1]), axis=0))

    def unit(high):
        return jnp.maximum(jnp.max(high, axis=0, keepdims=True) * (1.0 / TOP), TINY)

    def code(v, inv):
        return jnp.round(v * inv).astype(jnp.int32).astype(jnp.int16)

    def value(c, sc):
        return c.astype(jnp.int32).astype(f32) * sc

    SUB = 32

    def add_up(q):
        def weigh(r, c):
            at = pl.ds(pl.multiple_of(q * QW + r * SUB, SUB), SUB)
            w = x_buf[at, :] * fac[0:1, :]
            w_buf[pl.ds(pl.multiple_of(r * SUB, SUB), SUB), :] = w.astype(jnp.bfloat16)
            part = w[:, 0:128]
            for k in range(1, ROWS // 128):
                part = part + w[:, k * 128:(k + 1) * 128]
            mp[at, :] = part
            return c

        lax.fori_loop(0, QW // SUB, weigh, 0)
        swap = rem(q, 2)

        def tall(g, c):
            rows = pl.ds(pl.multiple_of(g * 384, 128), 384)
            y = lax.dot_general(et[rows, :], w_buf[...], NT, preferred_element_type=f32)
            for j in range(8):
                jx = g * 2 + j // 4
                jy = j % 4
                i0 = jx + swap * (jy - jx)
                i1 = jy + swap * (jx - jy)
                s_buf[q, i0, i1] = y[j * COLS:(j + 1) * COLS, :]
            return c

        lax.fori_loop(0, 2, tall, 0)
        a = place(q, 0)
        high = jnp.zeros((8, QW), f32)
        for k in range(1, SIDE):
            for j in range(SIDE):
                high = peak(s_buf[q, shift(a, k), j], high)
        sc = unit(high)
        sc1[q] = sc
        inv = 1.0 / sc
        for k in range(1, SIDE):
            for j in range(SIDE):
                s_q[q, shift(a, k), j] = code(s_buf[q, shift(a, k), j], inv)
        for copy in opening(q, 0):
            copy.start()

    def relay1(q):
        a = place(q, 0)
        for copy in opening(q, 0)[0:4]:
            copy.wait_recv()
        for way, lanes in ((0, la), (1, lb)):
            other_a = shift(a, 1 + 2 * way)
            sc = sc1r[q, way][:, lanes]
            high = jnp.zeros((8, 128), f32)
            for j in range(SIDE):
                v = value(rel1[q, way, j], sc) + s_buf[q, other_a, j][:, lanes]
                s_buf[q, other_a, j, :, lanes] = v
                high = peak(v, high)
            sc = unit(high)
            st1[q, way] = sc
            inv = 1.0 / sc
            for j in range(SIDE):
                tmp1[q, way, j] = code(s_buf[q, other_a, j][:, lanes], inv)
        for copy in closing(q, 0):
            copy.start()

    def close1(q):
        a = place(q, 0)
        b = place(q, 1)
        for copy in opening(q, 0)[4:6] + closing(q, 0):
            copy.wait_recv()
        high = jnp.zeros((8, QW), f32)
        for j in range(SIDE):
            j = shift(b, j)
            mine = s_buf[q, a, j]
            va = mine[:, la] + value(dir1[q, 1, j], sc1r[q, 1][:, la]) + value(rrl1[q, 0, j], st1r[q, 0])
            vb = mine[:, lb] + value(dir1[q, 0, j], sc1r[q, 0][:, lb]) + value(rrl1[q, 1, j], st1r[q, 1])
            v = jnp.concatenate([va, vb], axis=1)
            r1[q, j] = v
            high = peak(v, high)
        sc = unit(high)
        sc2[q] = sc
        inv = 1.0 / sc
        for k in range(1, SIDE):
            r_q[q, shift(b, k)] = code(r1[q, shift(b, k)], inv)
        for copy in opening(q, 1):
            copy.start()

    def relay2(q):
        b = place(q, 1)
        for copy in opening(q, 1)[0:4]:
            copy.wait_recv()
        for way, lanes in ((0, la), (1, lb)):
            v = value(rel2[q, way], sc2r[q, way][:, lanes]) + r1[q, shift(b, 1 + 2 * way)][:, lanes]
            sc = unit(peak(v, jnp.zeros((8, 128), f32)))
            st2[q, way] = sc
            tmp2[q, way] = code(v, 1.0 / sc)
        for copy in closing(q, 1):
            copy.start()

    def close2(q):
        b = place(q, 1)
        for copy in opening(q, 1)[4:6] + closing(q, 1):
            copy.wait_recv()
        mine = r1[q, b] + res[q]
        va = mine[:, la] + value(dir2[q, 1], sc2r[q, 1][:, la]) + value(rrl2[q, 0], st2r[q, 0])
        vb = mine[:, lb] + value(dir2[q, 0], sc2r[q, 0][:, lb]) + value(rrl2[q, 1], st2r[q, 1])
        lanes = pl.ds(pl.multiple_of(q * QW, QW), QW)
        out_ref[:, lanes] = jnp.concatenate([va, vb], axis=1) * mass[0:1, lanes]

    def mass_copy(src, dst, stage, k):
        along_x = 1 - stage
        nx = rem(px + k * along_x, SIDE)
        ny = rem(py + k * stage, SIDE)
        return pltpu.make_async_remote_copy(
            src_ref=src, dst_ref=dst.at[k], send_sem=m_send.at[stage * SIDE + k], recv_sem=m_recv.at[stage * SIDE + k],
            device_id=(nx * SIDE + ny, ce), device_id_type=MESH)

    def count():
        for k in range(NBLK):
            turned = jnp.transpose(mp[k * 128:(k + 1) * 128, :])
            mx[0, 0:1, k * 128:(k + 1) * 128] = jnp.sum(turned, axis=0, keepdims=True)
        for k in range(1, SIDE):
            mass_copy(mx.at[0], mx, 0, k).start()

    def count_x():
        for k in range(1, SIDE):
            mass_copy(mx.at[0], mx, 0, k).wait_recv()
        my[0] = (mx[0] + mx[1]) + (mx[2] + mx[3])
        for k in range(1, SIDE):
            mass_copy(my.at[0], my, 1, k).start()

    def count_y():
        for k in range(1, SIDE):
            mass_copy(my.at[0], my, 1, k).wait_recv()
        mass[...] = 1.0 / ((my[0] + my[1]) + (my[2] + my[3]) + 1.0)

    def old():
        pick_r = lax.broadcasted_iota(jnp.int32, (COLS, D), 0)
        pick_c = lax.broadcasted_iota(jnp.int32, (COLS, D), 1)
        pick = jnp.where(pick_c == pick_r + dp * COLS, 1.0, 0.0).astype(jnp.bfloat16)
        for b in range(QN):
            res[b] = lax.dot_general(pick, cent[b * QW:(b + 1) * QW, :], NT, preferred_element_type=f32)

    def turn(t, carry):
        @pl.when(t < QN)
        def _():
            add_up(t)

        @pl.when(t == QN - 1)
        def _():
            count()

        @pl.when((t >= 2) & (t < QN + 2))
        def _():
            relay1(t - 2)

        @pl.when(t == QN)
        def _():
            count_x()
            old()

        @pl.when((t >= 3) & (t < QN + 3))
        def _():
            close1(t - 3)

        @pl.when((t >= 4) & (t < QN + 4))
        def _():
            relay2(t - 4)

        @pl.when(t == 5)
        def _():
            count_y()

        @pl.when(t >= 5)
        def _():
            close2(t - 5)

        return carry

    lax.fori_loop(0, QN + 5, turn, 0)

    def sent_q(q, carry):
        for copy in opening(q, 0) + closing(q, 0) + opening(q, 1) + closing(q, 1):
            copy.wait_send()
        return carry

    lax.fori_loop(0, QN, sent_q, 0)
    for k in range(1, SIDE):
        mass_copy(mx.at[0], mx, 0, k).wait_send()
        mass_copy(my.at[0], my, 1, k).wait_send()

    def sent_z(i, carry):
        to_sibling(i, own).wait_send()
        for j in range(1, SIDE):
            give_stats(i, j).wait_send()

        @pl.when(i > 0)
        def _():
            for p in range(PIECES):
                hop(i, i, p, right).wait_send()
        return carry

    lax.fori_loop(0, Z, sent_z, 0)
    for k in range(3):
        share(k, 0).wait_send()
        share(k, 1).wait_send()
    share(3, 1 - core).wait_send()


def on_device(embeddings, candidates, centroids):
    f32, bf16, i16 = jnp.float32, jnp.bfloat16, jnp.int16
    dma = pltpu.SemaphoreType.DMA
    turned = pl.pallas_call(
        kernel,
        out_shape=jax.ShapeDtypeStruct((COLS, OWN), f32),
        in_specs=[pl.BlockSpec(memory_space=pl.ANY)] * 3,
        out_specs=pl.BlockSpec(memory_space=pltpu.VMEM),
        scratch_shapes=[
            pltpu.VMEM((Z, CHUNK, D), bf16),
            pltpu.VMEM((D, ROWS), bf16),
            pltpu.VMEM((OWN, D), bf16),
            pltpu.VMEM((NCAND, ROWS), jnp.int32),
            pltpu.VMEM((OWN, CHUNK), f32),
            pltpu.VMEM((OWN, ROWS), f32),
            pltpu.VMEM((QW, ROWS), bf16),
            pltpu.VMEM((8, 2 * CHUNK), f32),
            pltpu.VMEM((8, 2 * CHUNK), f32),
            pltpu.VMEM((Z, 2, CHUNK), f32),
            pltpu.VMEM((SIDE - 1, Z, 2, CHUNK), f32),
            pltpu.VMEM((Z, 2, CHUNK), f32),
            pltpu.VMEM((8, Z, 2, CHUNK), f32),
            pltpu.VMEM((Z, 1, CHUNK), f32),
            pltpu.VMEM((1, ROWS), f32),
            pltpu.VMEM((OWN, 128), f32),
            pltpu.VMEM((1, OWN), f32),
            pltpu.VMEM((SIDE, 1, OWN), f32),
            pltpu.VMEM((SIDE, 1, OWN), f32),
            pltpu.VMEM((QN, SIDE, SIDE, COLS, QW), f32),
            pltpu.VMEM((QN, SIDE, SIDE, COLS, QW), i16),
            pltpu.VMEM((QN, 2, SIDE, COLS, 128), i16),
            pltpu.VMEM((QN, 2, SIDE, COLS, 128), i16),
            pltpu.VMEM((QN, 2, SIDE, COLS, 128), i16),
            pltpu.VMEM((QN, 2, SIDE, COLS, 128), i16),
            pltpu.VMEM((QN, 1, QW), f32),
            pltpu.VMEM((QN, 2, 1, QW), f32),
            pltpu.VMEM((QN, 2, 1, 128), f32),
            pltpu.VMEM((QN, 2, 1, 128), f32),
            pltpu.VMEM((QN, SIDE, COLS, QW), f32),
            pltpu.VMEM((QN, SIDE, COLS, QW), i16),
            pltpu.VMEM((QN, 2, COLS, 128), i16),
            pltpu.VMEM((QN, 2, COLS, 128), i16),
            pltpu.VMEM((QN, 2, COLS, 128), i16),
            pltpu.VMEM((QN, 2, COLS, 128), i16),
            pltpu.VMEM((QN, 1, QW), f32),
            pltpu.VMEM((QN, 2, 1, QW), f32),
            pltpu.VMEM((QN, 2, 1, 128), f32),
            pltpu.VMEM((QN, 2, 1, 128), f32),
            pltpu.VMEM((QN, COLS, QW), f32),
            dma((3,)),
            dma((Z * PIECES,)), dma((Z * PIECES,)),
            dma((Z,)), dma((Z,)),
            dma(((SIDE - 1) * Z,)), dma(((SIDE - 1) * Z,)),
            dma((8,)), dma((8,)),
            dma((2 * SIDE,)), dma((2 * SIDE,)),
            dma((QN * 20,)), dma((QN * 20,)),
        ],
        compiler_params=pltpu.CompilerParams(
            collective_id=0, has_side_effects=True, vmem_limit_bytes=56 * 1024 * 1024),
    )(embeddings, jnp.transpose(candidates), centroids)
    return jnp.transpose(turned)


def solution(mesh):
    placed = (P(("dp", "cent"), None), P("dp", None), P("cent", None))
    return jax.shard_map(
        on_device, mesh=mesh, in_specs=placed, out_specs=P("cent", "dp"), check_vma=False
    )
```

time: 304 us -> 86.8 us (0.29)
  blocking collectives: 130 us -> 0 us
  waiting for transfers between devices: 128 us -> 0 us
  Pallas kernels: 0 us -> 83.5 us
  other arithmetic: 16.2 us -> 0 us
  matrix products: 14.4 us -> 0 us
  between operations: 13.5 us -> 0.01 us
    pallas_call x0 -> x1, Pallas kernels: none -> 83.5 us  [on_device(): pl.pallas_call(kernel, out_shape=jax.ShapeDtypeStruct((COLS, OWN), f32),...]
    psum x2 -> x0, blocking collectives: 80.5 us -> none  [the longest x1 46.8 us: on_device(): row_total = lax.psum(jnp.sum(exponent, axis=(1, 2)), 'cent')]
    all_gather x1 -> x0, waiting for transfers between devices: 76.2 us -> none  [on_device(): gathered = lax.all_gather(embeddings, 'cent', axis=0, tiled=True)]
    reduce_scatter x1 -> x0, waiting for transfers between devices: 50.7 us -> none  [on_device(): partial_sums = lax.psum_scatter(sums, 'dp', scatter_dimension=1, tiled=True)]
    pmax x1 -> x0, blocking collectives: 49.3 us -> none  [on_device(): row_max = lax.pmax(local_max, 'cent')]
    dot_general x2 -> x0, matrix products: 14.4 us -> none  [the longest x1 9.15 us: on_device(): lax.dot_general(gathered, centroids, (((1,), (1,)), ((), ())), preferred_...]
    reduce_sum x3 -> x0, other arithmetic: 11 us -> none  [the longest x1 5.76 us: on_device(): total_mass = lax.psum(jnp.sum(weights, axis=0), 'dp')]
  transfers between devices with their start and end apart: 2 -> 0, of which waited for: 2 -> 0; matrix products, arithmetic and copies ran while one was open for 2% -> 0% of each run, Pallas kernels for 0% -> 0%
where the time goes in v2:
time: 86.8 us; the launch traced here: 85.1 us
  Pallas kernels  83.5 us (96%)
  local copies, waits for them, and re-layouts  1.62 us (2%)
    pallas_call x1, Pallas kernels, on_device(): pl.pallas_call(kernel, out_shape=jax.ShapeDtypeStruct((COLS, OWN), f32),...  83.5 us

profile of v2, /device:TPU:6, one launch (start us, length us, event | category | flops | bytes accessed | tf_op | source)
XLA Modules:
  0.0 85.1 jit_solution(8691089669188787351)
XLA Ops:
  0.0 83.5 %shard_map.37 = f32[48,1024]{1,0:T(8,128)} custom-call(bf16[64,768]{1,0:T(8,128)(2,1)} %emb_hbm.1, s32[32,2048]{1,0:T(8,128)} %bitcast.3, bf16[1024,768]{1,0:T(8,128)(2,1)} %cent_hbm.1), custom_call_target="tpu_custom_call" | custom-call | tf_op jit(solution)/shard_map/pallas_call | solution.py:579
  83.5 1.6 %copy.5 = f32[1024,48]{0,1:T(8,128)} copy(f32[1024,48]{0,1:T(8,128)} %bitcast.2) | data formatting | bytes 393216

commit v3 on v2

v3 whole, which is shorter than its diff:
```python
import math

import jax
import jax.numpy as jnp
from jax import lax
from jax.experimental import pallas as pl
from jax.experimental.pallas import tpu as pltpu
from jax.sharding import PartitionSpec as P

D = 768
BLOCK = 128
Z = 16
SIDE = 4
SHARD = 64
CHUNK = 128
ROWS = Z * CHUNK
OWN = 1024
NBLK = OWN // BLOCK
COLS = 48
QN = 4
QW = OWN // QN
NCAND = 32
LOW = -1e30
FLOOR = -1e29
MESH = pl.DeviceIdType.MESH
NT = (((1,), (1,)), ((), ()))
PIECE = 16
PIECES = CHUNK // PIECE
HALF = PIECES // 2
HROWS = OWN // 2
NEAR = (1, -1, 2, -2)
STRIDE = (1, -1, 2, 0)
TOP = 32766.0
TINY = 1e-30


def rem(a, b):
    return lax.rem(a, b)


def kernel(emb_hbm, cand_hbm, cent_hbm, out_ref,
           e_all, et, cent, candt, hs, x_buf, w_buf, top_buf, tot_buf, st, sb, s2, s2r, fr, fac,
           mp, mass, mx, my, s_buf, s_q, rel1, dir1, rrl1, tmp1, sc1, sc1r, st1, st1r,
           r1, r_q, rel2, sc2, sc2r, res,
           in_sem, ag_send, ag_recv, la_send, la_recv, sib_send, sib_recv, st_send, st_recv, s2_send, s2_recv,
           m_send, m_recv, rs_send, rs_recv, ac_send, ac_recv):
    f32 = jnp.float32
    dp = lax.axis_index("dp")
    ce = lax.axis_index("cent")
    z = ce // 2
    core = rem(ce, 2)
    px = dp // SIDE
    py = rem(dp, SIDE)
    ahead = rem(z + 1 - 2 * core + Z, Z)
    own = pl.ds(pl.multiple_of(core * SHARD, SHARD), SHARD)

    load_e = pltpu.make_async_copy(emb_hbm, e_all.at[0, own], in_sem.at[0])
    load_c = pltpu.make_async_copy(cent_hbm, cent, in_sem.at[1])
    load_k = pltpu.make_async_copy(cand_hbm, candt, in_sem.at[2])
    load_e.start()
    load_c.start()
    load_k.start()

    barrier = pltpu.get_barrier_semaphore()

    def greet(d, c):
        pl.semaphore_signal(barrier, inc=1, device_id=(d, c), device_id_type=MESH)

    for c in range(2):
        for away in NEAR:
            greet(dp, rem(z + away + Z, Z) * 2 + c)
    greet(dp, z * 2 + 1 - core)
    for k in range(1, SIDE):
        greet(rem(px + k, SIDE) * SIDE + py, ce)
        greet(px * SIDE + rem(py + k, SIDE), ce)
    pl.semaphore_wait(barrier, 2 * len(NEAR) + 1 + 2 * (SIDE - 1))

    def rows_of(n):
        return pl.ds(pl.multiple_of(rem(n + HALF * core, PIECES) * PIECE, PIECE), PIECE)

    def hop(src, dst, n):
        return pltpu.make_async_remote_copy(
            src_ref=e_all.at[src, rows_of(n)], dst_ref=e_all.at[dst, rows_of(n)],
            send_sem=ag_send.at[dst * PIECES + n], recv_sem=ag_recv.at[dst * PIECES + n],
            device_id=(dp, ahead * 2 + core), device_id_type=MESH)

    def last(src, n):
        return pltpu.make_async_remote_copy(
            src_ref=e_all.at[src, rows_of(n)], dst_ref=e_all.at[Z - 1, rows_of(n)],
            send_sem=la_send.at[n], recv_sem=la_recv.at[n],
            device_id=(dp, ahead * 2 + 1 - core), device_id_type=MESH)

    other = pl.ds(pl.multiple_of((1 - core) * SHARD, SHARD), SHARD)

    def to_sibling(slot, half):
        rows = other if half else own
        return pltpu.make_async_remote_copy(
            src_ref=e_all.at[slot, rows], dst_ref=e_all.at[slot, rows],
            send_sem=sib_send.at[slot * 2 + half], recv_sem=sib_recv.at[slot * 2 + half],
            device_id=(dp, z * 2 + 1 - core), device_id_type=MESH)

    load_e.wait()
    to_sibling(0, 0).start()
    for n in range(HALF):
        hop(0, 1 + core, n).start()
    to_sibling(0, 0).wait_recv()
    for n in range(HALF, PIECES):
        hop(0, 1 + core, n).start()

    load_k.wait()
    load_c.wait()

    def square(b, carry):
        at = pl.ds(pl.multiple_of(b * BLOCK, BLOCK), BLOCK)
        c32 = cent[at, :].astype(f32)
        half = 0.5 * jnp.sum(c32 * c32, axis=1, keepdims=True)
        hs[at, :] = jnp.broadcast_to(half, (BLOCK, CHUNK))
        return carry

    lax.fori_loop(0, NBLK, square, 0)

    def source(i):
        odd = rem(i, 2)
        return rem(z + (1 - 2 * odd) * ((i + 1) // 2) + Z, Z)

    def give_stats(i, k, c):
        zs = source(i)
        return pltpu.make_async_remote_copy(
            src_ref=st.at[zs], dst_ref=sb.at[2 * k + core, zs],
            send_sem=st_send.at[2 * k + c], recv_sem=st_recv.at[2 * k + core],
            device_id=(dp, rem(z + STRIDE[k] + Z, Z) * 2 + c), device_id_type=MESH)

    def all_stats(k, c):
        return pltpu.make_async_remote_copy(
            src_ref=st, dst_ref=sb.at[2 * k + c], send_sem=st_send.at[2 * k + c], recv_sem=st_recv.at[2 * k + c],
            device_id=(dp, z * 2 + 1 - core), device_id_type=MESH)

    def tell(i):
        for k in range(3):
            give_stats(i, k, 0).start()
            give_stats(i, k, 1).start()
        give_stats(i, 3, 1 - core).start()

    scale = 1.0 / math.sqrt(D)

    def listed(i):
        return candt[:, pl.ds(pl.multiple_of(source(i) * CHUNK, CHUNK), CHUNK)]

    def logits(g, e, blocks, lanes, top):
        width = e.shape[0]
        dots = lax.dot_general(cent[g * HROWS:(g + 1) * HROWS, :], e, NT, preferred_element_type=f32)
        for k in range(HROWS // BLOCK):
            b = g * (HROWS // BLOCK) + k
            at = slice(b * BLOCK, (b + 1) * BLOCK)
            hit = jnp.max(jnp.where(blocks == ce * NBLK + b, 1.0, 0.0), axis=0, keepdims=True)
            h = hs[at, :]
            if width > CHUNK:
                h = jnp.concatenate([h, h], axis=1)
            l = jnp.where(hit > 0.5, (dots[k * BLOCK:(k + 1) * BLOCK, :] - h) * scale, LOW)
            x_buf[at, lanes] = l
            top = jnp.maximum(top, jnp.max(l.reshape(BLOCK // 8, 8, width), axis=0))
        return top

    def powers(g, m, lanes, total):
        width = m.shape[1]
        for k in range(HROWS // BLOCK):
            b = g * (HROWS // BLOCK) + k
            at = slice(b * BLOCK, (b + 1) * BLOCK)
            ex = jnp.exp(x_buf[at, lanes] - m)
            x_buf[at, lanes] = ex
            total = total + jnp.sum(ex.reshape(BLOCK // 8, 8, width), axis=0)
        return total

    def record(i, m, total):
        t = jnp.sum(total, axis=0, keepdims=True)
        for k in range(m.shape[1] // CHUNK):
            zs = source(i + k)
            st[zs, 0:1] = m[:, k * CHUNK:(k + 1) * CHUNK]
            st[zs, 1:2] = t[:, k * CHUNK:(k + 1) * CHUNK]
            tell(i + k)

    def turn_over(i):
        et[:, pl.ds(pl.multiple_of(i * CHUNK, CHUNK), CHUNK)] = jnp.transpose(e_all[i])

    def single(i):
        lanes = pl.ds(pl.multiple_of(i * CHUNK, CHUNK), CHUNK)
        e = e_all[i]
        top = jnp.full((8, CHUNK), FLOOR, f32)
        for g in range(2):
            top = logits(g, e, listed(i), lanes, top)
        m = jnp.max(top, axis=0, keepdims=True)
        total = jnp.zeros((8, CHUNK), f32)
        for g in range(2):
            total = powers(g, m, lanes, total)
        record(i, m, total)
        turn_over(i)

    def pair(u, part):
        i = 2 * u - 1
        lanes = pl.ds(pl.multiple_of(i * CHUNK, CHUNK), 2 * CHUNK)
        if part == 0:
            to_sibling(2 * u - core, 0).wait_recv()
            to_sibling(2 * u - core, 1).wait_recv()
        if part < 2:
            e = e_all[pl.ds(i, 2)].reshape(2 * CHUNK, D)
            blocks = jnp.concatenate([listed(i), listed(i + 1)], axis=1)
            top = jnp.full((8, 2 * CHUNK), FLOOR, f32) if part == 0 else top_buf[...]
            top = logits(part, e, blocks, lanes, top)
            if part == 1:
                top = jnp.broadcast_to(jnp.max(top, axis=0, keepdims=True), top.shape)
            top_buf[...] = top
        else:
            m = top_buf[0:1, :]
            total = jnp.zeros((8, 2 * CHUNK), f32) if part == 2 else tot_buf[...]
            total = powers(part - 2, m, lanes, total)
            turn_over(i + part - 2)
            if part == 2:
                tot_buf[...] = total
            else:
                record(i, m, total)

    def step(s, carry):
        slot = 2 * s - 1 + core
        for n in range(PIECES):
            @pl.when(s <= 7)
            def _():
                hop(slot, slot, n).wait_recv()
                if n < HALF:
                    hop(slot, jnp.minimum(slot + 2, Z - 1), n).start()

                    @pl.when(s == 7)
                    def _():
                        last(slot, n).start()
                else:
                    @pl.when(s <= 6)
                    def _():
                        hop(slot, slot + 2, n).start()

                if n == HALF - 1:
                    to_sibling(slot, 0).start()
                if n == PIECES - 1:
                    to_sibling(slot, 1).start()

            if n % 2 == 1:
                @pl.when((s >= 2) & (s <= 8))
                def _():
                    pair(s - 1, n // 2)

        @pl.when(s == 8)
        def _():
            for n in range(HALF):
                hop(Z - 1, Z - 1, n).wait_recv()
                last(Z - 1, n).wait_recv()

        @pl.when((s == 1) | (s == 8))
        def _():
            single(jnp.where(s == 1, 0, Z - 1))

        return carry

    lax.fori_loop(1, 9, step, 0)

    def merge(parts):
        big = parts[0][0]
        for m, _ in parts[1:]:
            big = jnp.maximum(big, m)
        tot = None
        for m, t in parts:
            term = t * jnp.exp(m - big)
            tot = term if tot is None else tot + term
        return big, tot

    def both(ref, *at):
        return ref[at + (slice(None), 0)], ref[at + (slice(None), 1)]

    for k in range(3):
        all_stats(k, 0).wait_recv()
        all_stats(k, 1).wait_recv()
    all_stats(3, 1 - core).wait_recv()
    big, tot = merge([both(st), both(sb, 6 + 1 - core)] + [both(sb, k) for k in range(6)])
    s2[:, 0, :] = big
    s2[:, 1, :] = tot

    def share(j):
        return pltpu.make_async_remote_copy(
            src_ref=s2, dst_ref=s2r.at[j - 1], send_sem=s2_send.at[j - 1], recv_sem=s2_recv.at[j - 1],
            device_id=(dp, rem(z + 4 * j, Z) * 2 + core), device_id_type=MESH)

    for j in (2, 1, 3):
        share(j).start()

    pick_r = lax.broadcasted_iota(jnp.int32, (COLS, D), 0)
    pick_c = lax.broadcasted_iota(jnp.int32, (COLS, D), 1)
    pick = jnp.where(pick_c == pick_r + dp * COLS, 1.0, 0.0).astype(jnp.bfloat16)
    for b in range(QN):
        res[b] = lax.dot_general(pick, cent[b * QW:(b + 1) * QW, :], NT, preferred_element_type=f32)

    def sent_z(s, carry):
        slot = 2 * s - 1 + core
        to_sibling(slot, 0).wait_send()
        to_sibling(slot, 1).wait_send()
        for n in range(PIECES):
            hop(slot, slot, n).wait_send()
        return carry

    lax.fori_loop(1, 8, sent_z, 0)
    to_sibling(0, 0).wait_send()
    for n in range(HALF):
        hop(Z - 1, Z - 1, n).wait_send()
        last(Z - 1, n).wait_send()
    for k in range(3):
        all_stats(k, 0).wait_send()
        all_stats(k, 1).wait_send()
    all_stats(3, 1 - core).wait_send()

    for j in (1, 3, 2):
        share(j).wait_recv()
    big, tot = merge([(big, tot)] + [both(s2r, j) for j in range(SIDE - 1)])
    fr[:, 0, :] = jnp.exp(st[:, 0, :] - big) / tot

    def factor(i, carry):
        fac[0:1, pl.ds(pl.multiple_of(i * CHUNK, CHUNK), CHUNK)] = fr[source(i)]
        return carry

    lax.fori_loop(0, Z, factor, 0)

    def neighbour(q, stage, way):
        along_x = rem(q + stage + 1, 2)
        along_y = 1 - along_x
        nx = rem(px + way * along_x + SIDE, SIDE)
        ny = rem(py + way * along_y + SIDE, SIDE)
        return (nx * SIDE + ny, ce)

    def place(q, stage):
        along_x = rem(q + stage + 1, 2)
        return px * along_x + py * (1 - along_x)

    def rs(src, dst, q, part, way):
        k = (q * 5 + part) * 2 + way
        return pltpu.make_async_remote_copy(
            src_ref=src, dst_ref=dst, send_sem=rs_send.at[k], recv_sem=rs_recv.at[k],
            device_id=neighbour(q, 0, 1 - 2 * way), device_id_type=MESH)

    la, lb = slice(0, 128), slice(128, 256)
    da, db = pl.ds(0, 128), pl.ds(128, 128)

    def shift(a, k):
        return rem(a + k, SIDE)

    def opening(q):
        a = place(q, 0)

        def piece(k, lanes):
            return s_q.at[q, shift(a, k), :, :, lanes]
        return [
            rs(sc1.at[q], sc1r.at[q, 0], q, 3, 0),
            rs(sc1.at[q], sc1r.at[q, 1], q, 3, 1),
            rs(piece(2, da), rel1.at[q, 0], q, 0, 0),
            rs(piece(2, db), rel1.at[q, 1], q, 0, 1),
            rs(piece(1, db), dir1.at[q, 0], q, 1, 0),
            rs(piece(3, da), dir1.at[q, 1], q, 1, 1),
        ]

    def closing(q):
        return [
            rs(st1.at[q, 0], st1r.at[q, 0], q, 4, 0),
            rs(st1.at[q, 1], st1r.at[q, 1], q, 4, 1),
            rs(tmp1.at[q, 0], rrl1.at[q, 0], q, 2, 0),
            rs(tmp1.at[q, 1], rrl1.at[q, 1], q, 2, 1),
        ]

    def across(q):
        b = place(q, 1)
        copies = []
        for k in (2, 1, 3):
            for n, (src, dst) in enumerate(((sc2.at[q], sc2r.at[q, k]), (r_q.at[q, shift(b, k)], rel2.at[q, k]))):
                copies.append(pltpu.make_async_remote_copy(
                    src_ref=src, dst_ref=dst, send_sem=ac_send.at[q * 8 + n * 4 + k], recv_sem=ac_recv.at[q * 8 + n * 4 + k],
                    device_id=neighbour(q, 1, k), device_id_type=MESH))
        return copies

    def peak(v, high):
        return jnp.maximum(high, jnp.max(jnp.abs(v).reshape(COLS // 8, 8, v.shape[1]), axis=0))

    def unit(high):
        return jnp.maximum(jnp.max(high, axis=0, keepdims=True) * (1.0 / TOP), TINY)

    def code(v, inv):
        return jnp.round(v * inv).astype(jnp.int32).astype(jnp.int16)

    def value(c, sc):
        return c.astype(jnp.int32).astype(f32) * sc

    SUB = 32

    def add_up(q):
        def weigh(r, c):
            at = pl.ds(pl.multiple_of(q * QW + r * SUB, SUB), SUB)
            w = x_buf[at, :] * fac[0:1, :]
            w_buf[pl.ds(pl.multiple_of(r * SUB, SUB), SUB), :] = w.astype(jnp.bfloat16)
            part = w[:, 0:128]
            for k in range(1, ROWS // 128):
                part = part + w[:, k * 128:(k + 1) * 128]
            mp[at, :] = part
            return c

        lax.fori_loop(0, QW // SUB, weigh, 0)
        swap = rem(q, 2)

        y = lax.dot_general(et[...], w_buf[...], NT, preferred_element_type=f32)
        for jx in range(SIDE):
            for jy in range(SIDE):
                i0 = jx + swap * (jy - jx)
                i1 = jy + swap * (jx - jy)
                j = (jx * SIDE + jy) * COLS
                s_buf[q, i0, i1] = y[j:j + COLS, :]
        a = place(q, 0)
        high = jnp.zeros((8, QW), f32)
        for k in range(1, SIDE):
            for j in range(SIDE):
                high = peak(s_buf[q, shift(a, k), j], high)
        sc = unit(high)
        sc1[q] = sc
        inv = 1.0 / sc
        for k in range(1, SIDE):
            for j in range(SIDE):
                s_q[q, shift(a, k), j] = code(s_buf[q, shift(a, k), j], inv)

    def relay1(q):
        a = place(q, 0)
        for copy in opening(q)[0:4]:
            copy.wait_recv()
        for way, lanes in ((0, la), (1, lb)):
            other_a = shift(a, 1 + 2 * way)
            sc = sc1r[q, way][:, lanes]
            high = jnp.zeros((8, 128), f32)
            for j in range(SIDE):
                v = value(rel1[q, way, j], sc) + s_buf[q, other_a, j][:, lanes]
                s_buf[q, other_a, j, :, lanes] = v
                high = peak(v, high)
            sc = unit(high)
            st1[q, way] = sc
            inv = 1.0 / sc
            for j in range(SIDE):
                tmp1[q, way, j] = code(s_buf[q, other_a, j][:, lanes], inv)
        for copy in closing(q):
            copy.start()

    def close1(q):
        a = place(q, 0)
        b = place(q, 1)
        for copy in opening(q)[4:6] + closing(q):
            copy.wait_recv()
        high = jnp.zeros((8, QW), f32)
        for j in range(SIDE):
            j = shift(b, j)
            mine = s_buf[q, a, j]
            va = mine[:, la] + value(dir1[q, 1, j], sc1r[q, 1][:, la]) + value(rrl1[q, 0, j], st1r[q, 0])
            vb = mine[:, lb] + value(dir1[q, 0, j], sc1r[q, 0][:, lb]) + value(rrl1[q, 1, j], st1r[q, 1])
            v = jnp.concatenate([va, vb], axis=1)
            r1[q, j] = v
            high = peak(v, high)
        sc = unit(high)
        sc2[q] = sc
        inv = 1.0 / sc
        for k in range(1, SIDE):
            r_q[q, shift(b, k)] = code(r1[q, shift(b, k)], inv)
        for copy in across(q):
            copy.start()

    def close2(q):
        b = place(q, 1)
        for copy in across(q):
            copy.wait_recv()
        total = r1[q, b] + res[q]
        for k in range(1, SIDE):
            total = total + value(rel2[q, k], sc2r[q, k])
        lanes = pl.ds(pl.multiple_of(q * QW, QW), QW)
        out_ref[:, lanes] = total * mass[0:1, lanes]

    def mass_copy(src, dst, stage, k):
        along_x = 1 - stage
        nx = rem(px + k * along_x, SIDE)
        ny = rem(py + k * stage, SIDE)
        return pltpu.make_async_remote_copy(
            src_ref=src, dst_ref=dst.at[k], send_sem=m_send.at[stage * SIDE + k], recv_sem=m_recv.at[stage * SIDE + k],
            device_id=(nx * SIDE + ny, ce), device_id_type=MESH)

    def count():
        for k in range(NBLK):
            turned = jnp.transpose(mp[k * 128:(k + 1) * 128, :])
            mx[0, 0:1, k * 128:(k + 1) * 128] = jnp.sum(turned, axis=0, keepdims=True)
        for k in range(1, SIDE):
            mass_copy(mx.at[0], mx, 0, k).start()

    def count_x():
        for k in range(1, SIDE):
            mass_copy(mx.at[0], mx, 0, k).wait_recv()
        my[0] = (mx[0] + mx[1]) + (mx[2] + mx[3])
        for k in range(1, SIDE):
            mass_copy(my.at[0], my, 1, k).start()

    def count_y():
        for k in range(1, SIDE):
            mass_copy(my.at[0], my, 1, k).wait_recv()
        mass[...] = 1.0 / ((my[0] + my[1]) + (my[2] + my[3]) + 1.0)

    def turn(t, carry):
        @pl.when(t < QN)
        def _():
            add_up(t)

        @pl.when((t >= 2) & (t < QN + 2))
        def _():
            relay1(t - 2)

        @pl.when(t < QN)
        def _():
            for copy in opening(t):
                copy.start()

        @pl.when(t == QN - 1)
        def _():
            count()

        @pl.when((t >= 3) & (t < QN + 3))
        def _():
            close1(t - 3)

        @pl.when(t == 5)
        def _():
            count_x()

        @pl.when(t == 6)
        def _():
            count_y()

        @pl.when(t >= 6)
        def _():
            close2(t - 6)

        return carry

    lax.fori_loop(0, QN + 6, turn, 0)

    def sent_q(q, carry):
        for copy in opening(q) + closing(q) + across(q):
            copy.wait_send()
        return carry

    lax.fori_loop(0, QN, sent_q, 0)
    for k in range(1, SIDE):
        mass_copy(mx.at[0], mx, 0, k).wait_send()
        mass_copy(my.at[0], my, 1, k).wait_send()
        share(k).wait_send()


def on_device(embeddings, candidates, centroids):
    f32, bf16, i16 = jnp.float32, jnp.bfloat16, jnp.int16
    dma = pltpu.SemaphoreType.DMA
    turned = pl.pallas_call(
        kernel,
        out_shape=pltpu.VMEM((COLS, OWN), f32),
        in_specs=[pl.BlockSpec(memory_space=pl.ANY)] * 3,
        out_specs=pl.BlockSpec(memory_space=pltpu.VMEM),
        scratch_shapes=[
            pltpu.VMEM((Z, CHUNK, D), bf16),
            pltpu.VMEM((D, ROWS), bf16),
            pltpu.VMEM((OWN, D), bf16),
            pltpu.VMEM((NCAND, ROWS), jnp.int32),
            pltpu.VMEM((OWN, CHUNK), f32),
            pltpu.VMEM((OWN, ROWS), f32),
            pltpu.VMEM((QW, ROWS), bf16),
            pltpu.VMEM((8, 2 * CHUNK), f32),
            pltpu.VMEM((8, 2 * CHUNK), f32),
            pltpu.VMEM((Z, 2, CHUNK), f32),
            pltpu.VMEM((8, Z, 2, CHUNK), f32),
            pltpu.VMEM((Z, 2, CHUNK), f32),
            pltpu.VMEM((SIDE - 1, Z, 2, CHUNK), f32),
            pltpu.VMEM((Z, 1, CHUNK), f32),
            pltpu.VMEM((1, ROWS), f32),
            pltpu.VMEM((OWN, 128), f32),
            pltpu.VMEM((1, OWN), f32),
            pltpu.VMEM((SIDE, 1, OWN), f32),
            pltpu.VMEM((SIDE, 1, OWN), f32),
            pltpu.VMEM((QN, SIDE, SIDE, COLS, QW), f32),
            pltpu.VMEM((QN, SIDE, SIDE, COLS, QW), i16),
            pltpu.VMEM((QN, 2, SIDE, COLS, 128), i16),
            pltpu.VMEM((QN, 2, SIDE, COLS, 128), i16),
            pltpu.VMEM((QN, 2, SIDE, COLS, 128), i16),
            pltpu.VMEM((QN, 2, SIDE, COLS, 128), i16),
            pltpu.VMEM((QN, 1, QW), f32),
            pltpu.VMEM((QN, 2, 1, QW), f32),
            pltpu.VMEM((QN, 2, 1, 128), f32),
            pltpu.VMEM((QN, 2, 1, 128), f32),
            pltpu.VMEM((QN, SIDE, COLS, QW), f32),
            pltpu.VMEM((QN, SIDE, COLS, QW), i16),
            pltpu.VMEM((QN, SIDE, COLS, QW), i16),
            pltpu.VMEM((QN, 1, QW), f32),
            pltpu.VMEM((QN, SIDE, 1, QW), f32),
            pltpu.VMEM((QN, COLS, QW), f32),
            dma((3,)),
            dma((Z * PIECES,)), dma((Z * PIECES,)),
            dma((HALF,)), dma((HALF,)),
            dma((2 * Z,)), dma((2 * Z,)),
            dma((8,)), dma((8,)),
            dma((SIDE,)), dma((SIDE,)),
            dma((2 * SIDE,)), dma((2 * SIDE,)),
            dma((QN * 10,)), dma((QN * 10,)),
            dma((QN * 8,)), dma((QN * 8,)),
        ],
        compiler_params=pltpu.CompilerParams(
            collective_id=0, has_side_effects=True, vmem_limit_bytes=56 * 1024 * 1024),
    )(embeddings, jnp.transpose(candidates), centroids)
    return jnp.transpose(turned)


def solution(mesh):
    placed = (P(("dp", "cent"), None), P("dp", None), P("cent", None))
    return jax.shard_map(
        on_device, mesh=mesh, in_specs=placed, out_specs=P("cent", "dp"), check_vma=False
    )
```

time: 86.8 us -> 74.7 us (0.86); the launches traced: 85.1 us -> 74 us
  Pallas kernels: 83.5 us -> 73.3 us
  local copies, waits for them, and re-layouts: 1.62 us -> 0.68 us
    pallas_call x1, Pallas kernels: 83.5 us -> 73.3 us  [on_device(): pl.pallas_call(kernel, out_shape=pltpu.VMEM((COLS, OWN), f32), in_specs=[...]
    unnamed x1, local copies, waits for them, and re-layouts: 1.62 us -> 0.68 us
where the time goes in v3:
time: 74.7 us; the launch traced here: 74 us
  Pallas kernels  73.3 us (98%)
    pallas_call x1, Pallas kernels, on_device(): pl.pallas_call(kernel, out_shape=pltpu.VMEM((COLS, OWN), f32), in_specs=[...  73.3 us

profile of v3, /device:TPU:6, one launch (start us, length us, event | category | flops | bytes accessed | tf_op | source)
XLA Modules:
  0.0 74.0 jit_solution(4283803757155264577)
XLA Ops:
  0.0 73.3 %shard_map.37 = f32[48,1024]{1,0:T(8,128)S(1)} custom-call(bf16[64,768]{1,0:T(8,128)(2,1)} %emb_hbm.1, s32[32,2048]{1,0:T(8,128)} %bitcast.3, bf16[1024,768]{1,0:T(8,128)(2,1)} %cent_hbm.1), custom_call_target="tpu_custom_call" | custom-call | tf_op jit(solution)/shard_map/pallas_call | solution.py:561
  73.3 0.7 copy.5

commit v4 on v3

--- a/solution.py
+++ b/solution.py
@@ -39,10 +39,10 @@
 
 
 def kernel(emb_hbm, cand_hbm, cent_hbm, out_ref,
-           e_all, et, cent, candt, hs, x_buf, w_buf, top_buf, tot_buf, st, sb, s2, s2r, fr, fac,
+           e_all, et, cent, candt, hs, x_buf, w_buf, top_buf, tot_buf, st, last_st, dbuf, sb, s2, s2r, fr, fac,
            mp, mass, mx, my, s_buf, s_q, rel1, dir1, rrl1, tmp1, sc1, sc1r, st1, st1r,
            r1, r_q, rel2, sc2, sc2r, res,
-           in_sem, ag_send, ag_recv, la_send, la_recv, sib_send, sib_recv, st_send, st_recv, s2_send, s2_recv,
+           in_sem, ag_send, ag_recv, la_send, la_recv, sib_send, sib_recv, st_send, st_recv, s2_send, s2_recv, db_send, db_recv,
            m_send, m_recv, rs_send, rs_recv, ac_send, ac_recv):
     f32 = jnp.float32
     dp = lax.axis_index("dp")
@@ -51,15 +51,9 @@
     core = rem(ce, 2)
     px = dp // SIDE
     py = rem(dp, SIDE)
+    facing = rem(z + Z // 2, Z)
     ahead = rem(z + 1 - 2 * core + Z, Z)
     own = pl.ds(pl.multiple_of(core * SHARD, SHARD), SHARD)
-
-    load_e = pltpu.make_async_copy(emb_hbm, e_all.at[0, own], in_sem.at[0])
-    load_c = pltpu.make_async_copy(cent_hbm, cent, in_sem.at[1])
-    load_k = pltpu.make_async_copy(cand_hbm, candt, in_sem.at[2])
-    load_e.start()
-    load_c.start()
-    load_k.start()
 
     barrier = pltpu.get_barrier_semaphore()
 
@@ -73,6 +67,13 @@
     for k in range(1, SIDE):
         greet(rem(px + k, SIDE) * SIDE + py, ce)
         greet(px * SIDE + rem(py + k, SIDE), ce)
+    load_e = pltpu.make_async_copy(emb_hbm, e_all.at[0, own], in_sem.at[0])
+    load_c = pltpu.make_async_copy(cent_hbm, cent, in_sem.at[1])
+    load_k = pltpu.make_async_copy(cand_hbm, candt, in_sem.at[2])
+    load_e.start()
+    load_c.start()
+    load_k.start()
+
     pl.semaphore_wait(barrier, 2 * len(NEAR) + 1 + 2 * (SIDE - 1))
 
     def rows_of(n):
@@ -192,7 +193,8 @@
         total = jnp.zeros((8, CHUNK), f32)
         for g in range(2):
             total = powers(g, m, lanes, total)
-        record(i, m, total)
+        last_st[0:1] = m
+        last_st[1:2] = jnp.sum(total, axis=0, keepdims=True)
         turn_over(i)
 
     def pair(u, part):
@@ -256,9 +258,38 @@
         def _():
             single(jnp.where(s == 1, 0, Z - 1))
 
+        @pl.when(s == 1)
+        def _():
+            st[z] = last_st[...]
+            tell(0)
+            st[facing, 0:1] = jnp.full((1, CHUNK), FLOOR, f32)
+            st[facing, 1:2] = jnp.zeros((1, CHUNK), f32)
+            tell(Z - 1)
+
         return carry
 
     lax.fori_loop(1, 9, step, 0)
+
+    def straight(dz, c):
+        return pltpu.make_async_remote_copy(
+            src_ref=last_st, dst_ref=dbuf.at[facing, core],
+            send_sem=db_send.at[dz * 2 + c], recv_sem=db_recv.at[facing * 2 + core],
+            device_id=(dp, rem(z + dz, Z) * 2 + c), device_id_type=MESH)
+
+    def come(k, c):
+        return pltpu.make_async_remote_copy(
+            src_ref=last_st, dst_ref=dbuf.at[k, c], send_sem=db_send.at[k * 2 + c], recv_sem=db_recv.at[k * 2 + c],
+            device_id=(dp, z * 2 + 1 - core), device_id_type=MESH)
+
+    def send_straight(m, carry):
+        dz = 8 + (1 - 2 * rem(m, 2)) * ((m + 1) // 2)
+        straight(dz, 0).start()
+        straight(dz, 1).start()
+        return carry
+
+    lax.fori_loop(0, Z - 1, send_straight, 0)
+    straight(0, 1 - core).start()
+    dbuf[facing, core] = last_st[...]
 
     def merge(parts):
         big = parts[0][0]
@@ -315,8 +346,20 @@
 
     for j in (1, 3, 2):
         share(j).wait_recv()
-    big, tot = merge([(big, tot)] + [both(s2r, j) for j in range(SIDE - 1)])
-    fr[:, 0, :] = jnp.exp(st[:, 0, :] - big) / tot
+
+    def take_straight(k, carry):
+        for c in range(2):
+            @pl.when((k != facing) | (core != c))
+            def _():
+                come(k, c).wait_recv()
+        return carry
+
+    lax.fori_loop(0, Z, take_straight, 0)
+    big, tot = merge(
+        [(big, tot)] + [both(s2r, j) for j in range(SIDE - 1)] + [(dbuf[:, c, 0, :], dbuf[:, c, 1, :]) for c in range(2)])
+    row = lax.broadcasted_iota(jnp.int32, (Z, CHUNK), 0)
+    mine = jnp.where(row == facing, last_st[0:1], st[:, 0, :])
+    fr[:, 0, :] = jnp.exp(mine - big) / tot
 
     def factor(i, carry):
         fac[0:1, pl.ds(pl.multiple_of(i * CHUNK, CHUNK), CHUNK)] = fr[source(i)]
@@ -394,17 +437,15 @@
     SUB = 32
 
     def add_up(q):
-        def weigh(r, c):
-            at = pl.ds(pl.multiple_of(q * QW + r * SUB, SUB), SUB)
-            w = x_buf[at, :] * fac[0:1, :]
-            w_buf[pl.ds(pl.multiple_of(r * SUB, SUB), SUB), :] = w.astype(jnp.bfloat16)
-            part = w[:, 0:128]
-            for k in range(1, ROWS // 128):
-                part = part + w[:, k * 128:(k + 1) * 128]
-            mp[at, :] = part
-            return c
-
-        lax.fori_loop(0, QW // SUB, weigh, 0)
+        for k in range(ROWS // QW):
+            cols = slice(k * QW, (k + 1) * QW)
+            f = fac[0:1, cols]
+            for r in range(QW // SUB):
+                at = pl.ds(pl.multiple_of(q * QW + r * SUB, SUB), SUB)
+                w = x_buf[at, cols] * f
+                w_buf[r * SUB:(r + 1) * SUB, cols] = w.astype(jnp.bfloat16)
+                part = w[:, 0:128] + w[:, 128:256]
+                mp[at, :] = part if k == 0 else mp[at, :] + part
         swap = rem(q, 2)
 
         y = lax.dot_general(et[...], w_buf[...], NT, preferred_element_type=f32)
@@ -510,9 +551,9 @@
         def _():
             add_up(t)
 
-        @pl.when((t >= 2) & (t < QN + 2))
-        def _():
-            relay1(t - 2)
+        @pl.when((t >= 3) & (t < QN + 3))
+        def _():
+            relay1(t - 3)
 
         @pl.when(t < QN)
         def _():
@@ -523,25 +564,25 @@
         def _():
             count()
 
-        @pl.when((t >= 3) & (t < QN + 3))
-        def _():
-            close1(t - 3)
-
-        @pl.when(t == 5)
+        @pl.when((t >= 6) & (t < QN + 6))
+        def _():
+            close1(t - 6)
+
+        @pl.when(t == 7)
         def _():
             count_x()
 
-        @pl.when(t == 6)
+        @pl.when(t == 9)
         def _():
             count_y()
 
-        @pl.when(t >= 6)
-        def _():
-            close2(t - 6)
-
-        return carry
-
-    lax.fori_loop(0, QN + 6, turn, 0)
+        @pl.when(t >= 9)
+        def _():
+            close2(t - 9)
+
+        return carry
+
+    lax.fori_loop(0, QN + 9, turn, 0)
 
     def sent_q(q, carry):
         for copy in opening(q) + closing(q) + across(q):
@@ -549,6 +590,13 @@
         return carry
 
     lax.fori_loop(0, QN, sent_q, 0)
+    def sent_straight(dz, carry):
+        straight(dz, 0).wait_send()
+        straight(dz, 1).wait_send()
+        return carry
+
+    lax.fori_loop(1, Z, sent_straight, 0)
+    straight(0, 1 - core).wait_send()
     for k in range(1, SIDE):
         mass_copy(mx.at[0], mx, 0, k).wait_send()
         mass_copy(my.at[0], my, 1, k).wait_send()
@@ -574,6 +622,8 @@
             pltpu.VMEM((8, 2 * CHUNK), f32),
             pltpu.VMEM((8, 2 * CHUNK), f32),
             pltpu.VMEM((Z, 2, CHUNK), f32),
+            pltpu.VMEM((2, CHUNK), f32),
+            pltpu.VMEM((Z, 2, 2, CHUNK), f32),
             pltpu.VMEM((8, Z, 2, CHUNK), f32),
             pltpu.VMEM((Z, 2, CHUNK), f32),
             pltpu.VMEM((SIDE - 1, Z, 2, CHUNK), f32),
@@ -605,6 +655,7 @@
             dma((2 * Z,)), dma((2 * Z,)),
             dma((8,)), dma((8,)),
             dma((SIDE,)), dma((SIDE,)),
+            dma((2 * Z,)), dma((2 * Z,)),
             dma((2 * SIDE,)), dma((2 * SIDE,)),
             dma((QN * 10,)), dma((QN * 10,)),
             dma((QN * 8,)), dma((QN * 8,)),

time: 74.7 us -> 72.6 us (0.972)
  Pallas kernels: 73.3 us -> 71.1 us
    pallas_call x1, Pallas kernels: 73.3 us -> 71.1 us  [on_device(): pl.pallas_call(kernel, out_shape=pltpu.VMEM((COLS, OWN), f32), in_specs=[...]
where the time goes in v4:
time: 72.6 us; the launch traced here: 71.8 us
  Pallas kernels  71.1 us (98%)
    pallas_call x1, Pallas kernels, on_device(): pl.pallas_call(kernel, out_shape=pltpu.VMEM((COLS, OWN), f32), in_specs=[...  71.1 us

profile of v4, /device:TPU:6, one launch (start us, length us, event | category | flops | bytes accessed | tf_op | source)
XLA Modules:
  0.0 71.8 jit_solution(18173359389924921894)
XLA Ops:
  0.0 71.1 %shard_map.37 = f32[48,1024]{1,0:T(8,128)S(1)} custom-call(bf16[64,768]{1,0:T(8,128)(2,1)} %emb_hbm.1, s32[32,2048]{1,0:T(8,128)} %bitcast.3, bf16[1024,768]{1,0:T(8,128)(2,1)} %cent_hbm.1), custom_call_target="tpu_custom_call" | custom-call | tf_op jit(solution)/shard_map/pallas_call | solution.py:609
  71.1 0.7 copy.5

commit v5 on v4

--- a/solution.py
+++ b/solution.py
@@ -557,7 +557,12 @@
 
         @pl.when(t < QN)
         def _():
-            for copy in opening(t):
+            for copy in opening(t)[0:4]:
+                copy.start()
+
+        @pl.when((t >= 1) & (t < QN + 1))
+        def _():
+            for copy in opening(t - 1)[4:6]:
                 copy.start()
 
         @pl.when(t == QN - 1)

time: 72.6 us -> 72.7 us (level)
  no operation moved by 1% of the time
where the time goes in v5:
time: 72.7 us; the launch traced here: 72.1 us
  Pallas kernels  71.4 us (98%)
    pallas_call x1, Pallas kernels, on_device(): pl.pallas_call(kernel, out_shape=pltpu.VMEM((COLS, OWN), f32), in_specs=[...  71.4 us

profile of v5, /device:TPU:6, one launch (start us, length us, event | category | flops | bytes accessed | tf_op | source)
XLA Modules:
  0.0 72.1 jit_solution(17125239155318718833)
XLA Ops:
  0.0 71.4 %shard_map.37 = f32[48,1024]{1,0:T(8,128)S(1)} custom-call(bf16[64,768]{1,0:T(8,128)(2,1)} %emb_hbm.1, s32[32,2048]{1,0:T(8,128)} %bitcast.3, bf16[1024,768]{1,0:T(8,128)(2,1)} %cent_hbm.1), custom_call_target="tpu_custom_call" | custom-call | tf_op jit(solution)/shard_map/pallas_call | solution.py:614
  71.4 0.7 copy.5
